TPU v7x, 256 devices: a whole 4x4x8 slice. The times are simulated.
256 devices in a mesh: slab: 16 (over y, z_hi), filt: 16 (over x, z_lo, core).
Axes of the slice: x: 4, y: 4, z: 8 (z_hi: 4, z_lo: 2; z = z_hi * 2 + z_lo), core: 2. Of those that a mesh axis runs over, the one named last changes fastest.
Arguments:
- cotangent: bfloat16 [32, 16, 64, 256], P('slab', None, None, 'filt'), may hold values from -6 to 6
- pre_act: bfloat16 [32, 16, 64, 256], P('slab', 'filt'), may hold values from -6 to 6
- layer_input: bfloat16 [32, 16, 64, 128], P('slab', 'filt'), may hold values from -6 to 6
- weight_one: bfloat16 [27, 128, 256], replicated, may hold values from -0.078125 to 0.078125
- weight_two: bfloat16 [27, 256, 256], P(None, None, 'filt'), may hold values from -0.078125 to 0.078125
Outputs:
- grad_w2: float32 [27, 256, 256], P(None, None, 'filt')
- grad_w1: float32 [27, 128, 256], replicated
- grad_x0: bfloat16 [32, 16, 64, 128], P('slab', 'filt')
All inputs are finite; a program needn't handle non-finite values.
Results may differ from a plain program's by a relative error of at most 0.0013.
Values may be sent and summed in bfloat16 or wider, within the bound.
No kernel may reach another device: no remote copies, remote signals or barrier semaphores. Data moves between devices by JAX's collectives and lax.ppermute only.
A program may use at most 128 MiB of HBM per device.

v0:
```python
import math

import jax
import jax.numpy as jnp
from jax import lax
from jax.sharding import PartitionSpec as P

leak_slope = 0.3


def padded(block, sides, width):
    for axis, dim in sides:
        count = lax.axis_size(axis)
        forward = [(i, i + 1) for i in range(count - 1)]
        backward = [(target, source) for source, target in forward]
        low = lax.ppermute(
            lax.slice_in_dim(block, block.shape[dim] - width, None, axis=dim), axis, forward
        )
        high = lax.ppermute(lax.slice_in_dim(block, 0, width, axis=dim), axis, backward)
        block = jnp.concatenate([low, block, high], axis=dim)
    return block


def tap_offsets():
    return [(a, b, c) for a in (-1, 0, 1) for b in (-1, 0, 1) for c in (-1, 0, 1)]


def leaky_relu(value):
    return jnp.where(value > 0, value, leak_slope * value)


def relu_slope(value):
    return jnp.where(value > 0, jnp.float32(1.0), jnp.float32(leak_slope))


def pad_columns(field):
    return jnp.pad(field, ((0, 0), (0, 0), (1, 1), (0, 0)))


def backward_columns(framed, planes_here, row_count, col_count):
    pieces = [
        framed[1 - a : 1 - a + planes_here, 1 - b : 1 - b + row_count, 1 - c : 1 - c + col_count]
        for a, b, c in tap_offsets()
    ]
    return jnp.concatenate(pieces, axis=-1)


def forward_columns(framed, planes_here, row_count, col_count):
    pieces = [
        framed[1 + a : 1 + a + planes_here, 1 + b : 1 + b + row_count, 1 + c : 1 + c + col_count]
        for a, b, c in tap_offsets()
    ]
    return jnp.concatenate(pieces, axis=-1)


def shards(cotangent, pre_act, layer_input, weight_one, weight_two):
    planes_here, row_count, col_count, out_local = cotangent.shape
    rows_here = pre_act.shape[1]
    mid_width = weight_two.shape[1]
    in_width = weight_one.shape[1]
    n_slab = lax.axis_size("slab")
    grad_scale = jnp.float32(1.0 / math.sqrt(planes_here * n_slab * row_count * col_count))
    activation = leaky_relu(pre_act.astype(jnp.float32)).astype(jnp.bfloat16)
    gathered = lax.all_gather(activation, "filt", axis=1, tiled=True)
    framed = padded(gathered, (("slab", 0),), 1)
    framed = jnp.pad(framed, ((0, 0), (1, 1), (1, 1), (0, 0)))
    wide_cot = jnp.pad(cotangent, ((2, 2), (2, 2), (2, 2), (0, 0)))
    shifted = jnp.concatenate(
        [
            wide_cot[
                1 - a : 3 - a + planes_here, 1 - b : 3 - b + row_count, 1 - c : 3 - c + col_count
            ]
            for a, b, c in tap_offsets()
        ],
        axis=-1,
    )
    local_two = jnp.einsum("dhwc,dhwk->ck", framed, shifted, preferred_element_type=jnp.float32)
    local_two = local_two.reshape(mid_width, 27, out_local).transpose(1, 0, 2) * grad_scale
    grad_w2 = lax.psum(local_two, "slab")
    cot_rim = padded(cotangent, (("slab", 0),), 1)
    weight_mat = weight_two.transpose(0, 2, 1).reshape(27 * out_local, mid_width)
    rows_first = jnp.pad(cot_rim, ((0, 0), (1, 1), (1, 1), (0, 0))).transpose(1, 0, 2, 3)
    pieces = [
        rows_first[
            1 - b : 1 - b + row_count, 1 - a : 1 - a + planes_here, 1 - c : 1 - c + col_count
        ]
        for a, b, c in tap_offsets()
    ]
    cot_cols = jnp.concatenate(pieces, axis=-1)
    whole_term = jnp.einsum(
        "hdwk,kc->hdwc", cot_cols, weight_mat, preferred_element_type=jnp.float32
    )
    summed = lax.psum_scatter(whole_term, "filt", scatter_dimension=3, tiled=True)
    own_sums = lax.all_to_all(summed, "filt", split_axis=0, concat_axis=3, tiled=True)
    back_sum = own_sums.transpose(1, 0, 2, 3)
    error_signal = back_sum * relu_slope(pre_act.astype(jnp.float32))
    input_frame = padded(layer_input, (("slab", 0), ("filt", 1)), 1)
    input_frame = pad_columns(input_frame)
    input_cols = forward_columns(input_frame, planes_here, rows_here, col_count).astype(jnp.float32)
    local_one = jnp.einsum(
        "dhwk,dhwc->kc",
        input_cols,
        error_signal,
        preferred_element_type=jnp.float32,
        precision=lax.Precision.HIGHEST,
    )
    local_one = local_one.reshape(27, in_width, mid_width) * grad_scale
    grad_w1 = lax.psum(local_one, ("slab", "filt"))
    error_frame = padded(error_signal, (("slab", 0), ("filt", 1)), 1)
    error_frame = pad_columns(error_frame)
    error_cols = backward_columns(error_frame, planes_here, rows_here, col_count)
    first_mat = weight_one.astype(jnp.float32).transpose(0, 2, 1).reshape(27 * mid_width, in_width)
    grad_x0 = jnp.einsum(
        "dhwk,kc->dhwc",
        error_cols,
        first_mat,
        preferred_element_type=jnp.float32,
        precision=lax.Precision.HIGHEST,
    ).astype(jnp.bfloat16)
    return (grad_w2, grad_w1, grad_x0)


def solution(mesh):
    return jax.shard_map(
        shards,
        mesh=mesh,
        in_specs=(
            P("slab", None, None, "filt"),
            P("slab", "filt", None, None),
            P("slab", "filt", None, None),
            P(),
            P(None, None, "filt"),
        ),
        out_specs=(P(None, None, "filt"), P(), P("slab", "filt", None, None)),
        check_vma=False,
    )
```

profile of v0, /device:TPU:2, one launch (start us, length us, event | category | flops | bytes accessed | tf_op | source)
XLA Modules:
  0.0 650.2 jit_solution(14180263789711778437)
XLA Ops:
  9.5 5.8 collective-permute-start.6
  16.0 6.4 collective-permute-start.2
  24.9 11.0 %pad_slice_fusion = (bf16[4,18,66,16]{3,2,1,0:T(8,128)(2,1)}, bf16[4,18,66,16]{3,2,1,0:T(8,128)(2,1)}, bf16[4,18,66,16]{3,2,1,0:T(8,128)(2,1)}, bf16[4,18,66,16]...) fusion(bf16[2,16,64,16]{3,2,1,0:T(8,128)(2,1)S(1)} %copy.23), kind=kLoop, calls=%fused_computation | loop fusion | bytes 2954752 | tf_op jit(solution)/shard_map/slice | solution.py:70
  39.8 2.3 collective-permute-start.4
  45.2 4.4 fusion.49
  49.6 11.9 %concatenate.50 = bf16[16,2,64,432]{3,2,1,0:T(8,128)(2,1)S(1)} concatenate(bf16[16,2,64,16]{3,2,1,0:T(8,128)(2,1)} %get-tuple-element.38, bf16[16,2,64,16]{3,2,1,0:T(8,128)(2,1)} %get-tuple-element.37, bf16[16,2,64,16]{3,2,1,0:T(8,128)(2,1)} %get-tuple-element.36, bf16[16,2,64,16]{3,2,1,0:T(8,128)(2,1)} %get-tuple-element.35, bf16[16,2,64,16]{3,2,1,0:T(8,128)(2,1)} %get-tuple-element.34, ...), dimensions={3} | concatenate | bytes 3538944 | tf_op jit(solution)/shard_map/concatenate | solution.py:89
  61.6 3.3 fusion.55
  65.0 5.5 pad_slice_fusion.1
  70.4 2.8 copy.28
  73.2 32.1 %concatenate.43 = bf16[4,18,66,432]{3,2,1,0:T(8,128)(2,1)} concatenate(bf16[4,18,66,16]{3,2,1,0:T(8,128)(2,1)} %get-tuple-element.67, bf16[4,18,66,16]{3,2,1,0:T(8,128)(2,1)} %get-tuple-element.42, bf16[4,18,66,16]{3,2,1,0:T(8,128)(2,1)} %get-tuple-element.43, bf16[4,18,66,16]{3,2,1,0:T(8,128)(2,1)} %get-tuple-element.44, bf16[4,18,66,16]{3,2,1,0:T(8,128)(2,1)} %get-tuple-element.45, ...), dimensions={3} | concatenate | bytes 8211456 | tf_op jit(solution)/shard_map/concatenate | solution.py:68
  117.4 15.7 %reduce-scatter.2.cloned.1.call-done = f32[16,2,64,16]{2,3,1,0:T(8,128)} async-done(((f32[16,2,64,256]{2,3,1,0:T(8,128)}), f32[16,2,64,16]{2,3,1,0:T(8,128)}) %reduce-scatter.2.cloned.1.call-update) | async-done | bytes 131088 | tf_op jit(solution)/shard_map/reduce_scatter | solution.py:93
  134.9 11.1 %all-to-all-start = ((f32[16,1,2048]{2,1,0:T(1,128)}), f32[16,1,2048]{2,1,0:T(1,128)S(1)}, u32[]{:S(2)}, u32[]{:S(2)}) async-start(f32[16,1,2048]{2,1,0:T(1,128)} %reshape.39), calls=%async_computation.1 | async-start | bytes 262144 | tf_op jit(solution)/shard_map/all_to_all | solution.py:94
  147.3 3.6 all-to-all-done
  158.5 5.6 collective-permute-start.8
  165.9 2.3 collective-permute-start.11
  170.2 4.6 bitcast_multiply_fusion
  174.9 3.8 collective-permute-done.10
  197.2 6.0 collective-permute-start
  205.3 19.4 %collective-permute-done.1 = bf16[1,16,64,256]{3,2,1,0:T(8,128)(2,1)S(1)} collective-permute-done((bf16[1,16,64,256]{3,2,1,0:T(8,128)(2,1)S(1)}, bf16[1,16,64,256]{3,2,1,0:T(8,128)(2,1)S(1)}, u32[]{:S(2)}, u32[]{:S(2)}) %collective-permute-start.1) | collective-permute-done | bytes 524320 | tf_op jit(solution)/shard_map/ppermute | solution.py:19
  224.7 6.0 fusion.23
  231.4 4.5 fusion.27
  235.9 235.8 %all-reduce.10.cloned.1.call-done = f32[27,128,256]{2,1,0:T(8,128)} async-done(((f32[27,128,256]{2,1,0:T(8,128)}), f32[27,128,256]{2,1,0:T(8,128)}) %all-reduce.10.cloned.1.call-update) | async-done | bytes 3538960 | tf_op jit(solution)/shard_map/psum | solution.py:108
  471.7 166.0 %all-reduce.8.cloned.1.call-done = f32[27,256,16]{1,2,0:T(8,128)} async-done(((f32[27,256,16]{1,2,0:T(8,128)}), f32[27,256,16]{1,2,0:T(8,128)}) %all-reduce.8.cloned.1.call-update) | async-done | bytes 442384 | tf_op jit(solution)/shard_map/psum | solution.py:79
  639.5 4.2 copy.95
  (119 shorter events, 62.0 us)
Async XLA Ops:
  7.2 54.4 %copy-start = (bf16[27,256,16]{1,2,0:T(8,128)(2,1)S(1)}, bf16[27,256,16]{1,2,0:T(8,128)(2,1)}, u32[]{:S(2)}) copy-start(bf16[27,256,16]{1,2,0:T(8,128)(2,1)} %param.9) | copy-start | bytes 663556
  7.2 126.0 %reduce-scatter.2.cloned.1.call-start = ((), (), s32[]{:S(2)}) async-start(), calls=%async_computation.4 | async-start | bytes 4456448 | tf_op jit(solution)/shard_map/reduce_scatter | solution.py:93
  8.2 33.9 %collective-permute-start.7 = (bf16[1,16,64,16]{2,3,1,0:T(8,128)(2,1)S(1)}, bf16[1,16,64,16]{2,3,1,0:T(8,128)(2,1)S(1)}, u32[]{:S(2)}, u32[]{:S(2)}) collective-permute-start(bf16[1,16,64,16]{2,3,1,0:T(8,128)(2,1)S(1)} %get-tuple-element.71), channel_id=1, source_target_pairs={{16,0},{32,16},{48,32},{64,48},{80,64},{96,80},{112,96},{128,112},... | collective-permute-start | bytes 98312 | tf_op jit(solution)/shard_map/ppermute | solution.py:19
  9.5 32.6 %collective-permute-start.6 = (bf16[1,16,64,16]{2,3,1,0:T(8,128)(2,1)S(1)}, bf16[1,16,64,16]{2,3,1,0:T(8,128)(2,1)S(1)}, u32[]{:S(2)}, u32[]{:S(2)}) collective-permute-start(bf16[1,16,64,16]{2,3,1,0:T(8,128)(2,1)S(1)} %get-tuple-element.70), channel_id=1, source_target_pairs={{0,16},{16,32},{32,48},{48,64},{64,80},{80,96},{96,112},{112,128},... | collective-permute-start | bytes 98312 | tf_op jit(solution)/shard_map/ppermute | solution.py:16
  16.0 19.9 %collective-permute-start.2 = (bf16[1,1,64,128]{3,2,1,0:T(8,128)(2,1)S(1)}, bf16[1,1,64,128]{3,2,1,0:T(8,128)(2,1)S(1)}, u32[]{:S(2)}, u32[]{:S(2)}) collective-permute-start(bf16[1,1,64,128]{3,2,1,0:T(8,128)(2,1)S(1)} %get-tuple-element.75), channel_id=1, source_target_pairs={{0,16},{16,32},{32,48},{48,64},{64,80},{80,96},{96,112},{112,128},... | collective-permute-start | bytes 49160 | tf_op jit(solution)/shard_map/ppermute | solution.py:16
  22.4 14.7 %collective-permute-start.3 = (bf16[1,1,64,128]{3,2,1,0:T(8,128)(2,1)S(1)}, bf16[1,1,64,128]{3,2,1,0:T(8,128)(2,1)S(1)}, u32[]{:S(2)}, u32[]{:S(2)}) collective-permute-start(bf16[1,1,64,128]{3,2,1,0:T(8,128)(2,1)S(1)} %get-tuple-element.74), channel_id=1, source_target_pairs={{16,0},{32,16},{48,32},{64,48},{80,64},{96,80},{112,96},{128,112},... | collective-permute-start | bytes 49160 | tf_op jit(solution)/shard_map/ppermute | solution.py:19
  24.9 11.6 %copy-start.4 = (bf16[2,1,64,128]{3,2,1,0:T(8,128)(2,1)S(1)}, bf16[2,1,64,128]{3,2,1,0:T(8,128)(2,1)}, u32[]{:S(2)}) copy-start(bf16[2,1,64,128]{3,2,1,0:T(8,128)(2,1)} %param.7) | copy-start | bytes 98308
  24.9 17.2 %copy-start.2 = (bf16[2,16,64,16]{2,3,1,0:T(8,128)(2,1)S(1)}, bf16[2,16,64,16]{2,3,1,0:T(8,128)(2,1)}, u32[]{:S(2)}) copy-start(bf16[2,16,64,16]{2,3,1,0:T(8,128)(2,1)} %param.5) | copy-start | bytes 196612
  37.7 67.5 %collective-permute-start.5 = (bf16[4,1,64,128]{3,2,1,0:T(8,128)(2,1)}, bf16[4,1,64,128]{3,2,1,0:T(8,128)(2,1)S(1)}, u32[]{:S(2)}, u32[]{:S(2)}) collective-permute-start(bf16[4,1,64,128]{3,2,1,0:T(8,128)(2,1)} %constant_dynamic-update-slice_fusion), channel_id=1, source_target_pairs={{1,0},{2,1},{3,2},{4,3},{5,4},{6,5},{7,6},{8,7},{9,8},{10,9},{11,1... | collective-permute-start | bytes 196616 | tf_op jit(solution)/shard_map/ppermute | solution.py:19
  39.8 65.5 %collective-permute-start.4 = (bf16[4,1,64,128]{3,2,1,0:T(8,128)(2,1)}, bf16[4,1,64,128]{3,2,1,0:T(8,128)(2,1)S(1)}, u32[]{:S(2)}, u32[]{:S(2)}) collective-permute-start(bf16[4,1,64,128]{3,2,1,0:T(8,128)(2,1)} %constant_dynamic-update-slice_fusion), channel_id=1, source_target_pairs={{0,1},{1,2},{2,3},{3,4},{4,5},{5,6},{6,7},{7,8},{8,9},{9,10},{10,1... | collective-permute-start | bytes 196616 | tf_op jit(solution)/shard_map/ppermute | solution.py:16
  73.2 35.5 %copy-start.6 = (bf16[1,1,64,128]{3,2,1,0:T(8,128)(2,1)S(1)}, bf16[1,1,64,128]{3,2,1,0:T(8,128)(2,1)}, u32[]{:S(2)}) copy-start(bf16[1,1,64,128]{3,2,1,0:T(8,128)(2,1)} %copy-done.5) | copy-start | bytes 49156
  105.3 47.5 %copy-start.7 = (bf16[2,1,64,256]{3,2,1,0:T(8,128)(2,1)S(1)}, bf16[2,1,64,256]{3,2,1,0:T(8,128)(2,1)}, u32[]{:S(2)}) copy-start(bf16[2,1,64,256]{3,2,1,0:T(8,128)(2,1)} %param.6) | copy-start | bytes 196612
  134.9 16.0 %all-to-all-start = ((f32[16,1,2048]{2,1,0:T(1,128)}), f32[16,1,2048]{2,1,0:T(1,128)S(1)}, u32[]{:S(2)}, u32[]{:S(2)}) async-start(f32[16,1,2048]{2,1,0:T(1,128)} %reshape.39), calls=%async_computation.1 | async-start | bytes 262144 | tf_op jit(solution)/shard_map/all_to_all | solution.py:94
  146.0 48.5 %all-gather.2.cloned.1.call-start = ((), (), s32[]{:S(2)}) async-start(), calls=%async_computation.2 | async-start | bytes 1114112 | tf_op jit(solution)/shard_map/all_gather | solution.py:64
  153.4 318.3 %all-reduce.10.cloned.1.call-start = ((), (), s32[]{:S(2)}) async-start(), calls=%async_computation.5 | async-start | bytes 7077888 | tf_op jit(solution)/shard_map/psum | solution.py:108
  157.2 8.5 %collective-permute-start.9 = (f32[1,1,64,256]{3,2,1,0:T(8,128)S(1)}, f32[1,1,64,256]{3,2,1,0:T(8,128)S(1)}, u32[]{:S(2)}, u32[]{:S(2)}) collective-permute-start(f32[1,1,64,256]{3,2,1,0:T(8,128)S(1)} %get-tuple-element.69), channel_id=1, source_target_pairs={{16,0},{32,16},{48,32},{64,48},{80,64},{96,80},{112,96},{128,112},... | collective-permute-start | bytes 196616 | tf_op jit(solution)/shard_map/ppermute | solution.py:19
  158.5 7.3 %collective-permute-start.8 = (f32[1,1,64,256]{3,2,1,0:T(8,128)S(1)}, f32[1,1,64,256]{3,2,1,0:T(8,128)S(1)}, u32[]{:S(2)}, u32[]{:S(2)}) collective-permute-start(f32[1,1,64,256]{3,2,1,0:T(8,128)S(1)} %get-tuple-element.68), channel_id=1, source_target_pairs={{0,16},{16,32},{32,48},{48,64},{64,80},{80,96},{96,112},{112,128},... | collective-permute-start | bytes 196616 | tf_op jit(solution)/shard_map/ppermute | solution.py:16
  165.9 9.0 %collective-permute-start.11 = (f32[4,1,64,256]{3,2,1,0:T(8,128)S(1)}, f32[4,1,64,256]{3,2,1,0:T(8,128)S(1)}, u32[]{:S(2)}, u32[]{:S(2)}) collective-permute-start(f32[4,1,64,256]{3,2,1,0:T(8,128)S(1)} %pad_maximum_fusion.1), channel_id=1, source_target_pairs={{1,0},{2,1},{3,2},{4,3},{5,4},{6,5},{7,6},{8,7},{9,8},{10,9},{11,1... | collective-permute-start | bytes 786440 | tf_op jit(solution)/shard_map/ppermute | solution.py:19
  168.2 10.4 %collective-permute-start.10 = (f32[4,1,64,256]{3,2,1,0:T(8,128)S(1)}, f32[4,1,64,256]{3,2,1,0:T(8,128)S(1)}, u32[]{:S(2)}, u32[]{:S(2)}) collective-permute-start(f32[4,1,64,256]{3,2,1,0:T(8,128)S(1)} %pad_maximum_fusion.1), channel_id=1, source_target_pairs={{0,1},{1,2},{2,3},{3,4},{4,5},{5,6},{6,7},{7,8},{8,9},{9,10},{10,1... | collective-permute-start | bytes 786440 | tf_op jit(solution)/shard_map/ppermute | solution.py:16
  174.8 462.8 %all-reduce.8.cloned.1.call-start = ((), (), s32[]{:S(2)}) async-start(), calls=%async_computation.3 | async-start | bytes 884736 | tf_op jit(solution)/shard_map/psum | solution.py:79
  194.5 30.2 %copy-start.3 = (bf16[2,16,64,256]{3,2,1,0:T(8,128)(2,1)S(1)}, bf16[2,16,64,256]{3,2,1,0:T(8,128)(2,1)}, u32[]{:S(2)}) copy-start(bf16[2,16,64,256]{3,2,1,0:T(8,128)(2,1)} %all-gather.2.cloned.1.call-done) | copy-start | bytes 3145732
  195.9 28.8 %collective-permute-start.1 = (bf16[1,16,64,256]{3,2,1,0:T(8,128)(2,1)S(1)}, bf16[1,16,64,256]{3,2,1,0:T(8,128)(2,1)S(1)}, u32[]{:S(2)}, u32[]{:S(2)}) collective-permute-start(bf16[1,16,64,256]{3,2,1,0:T(8,128)(2,1)S(1)} %get-tuple-element.40), channel_id=1, source_target_pairs={{16,0},{32,16},{48,32},{64,48},{80,64},{96,80},{112,96},{128,112},... | collective-permute-start | bytes 1572872 | tf_op jit(solution)/shard_map/ppermute | solution.py:19
  197.2 27.5 %collective-permute-start = (bf16[1,16,64,256]{3,2,1,0:T(8,128)(2,1)S(1)}, bf16[1,16,64,256]{3,2,1,0:T(8,128)(2,1)S(1)}, u32[]{:S(2)}, u32[]{:S(2)}) collective-permute-start(bf16[1,16,64,256]{3,2,1,0:T(8,128)(2,1)S(1)} %get-tuple-element.39), channel_id=1, source_target_pairs={{0,16},{16,32},{32,48},{48,64},{64,80},{80,96},{96,112},{112,128},... | collective-permute-start | bytes 1572872 | tf_op jit(solution)/shard_map/ppermute | solution.py:16
  637.6 6.0 copy-start.1
  (1 other events, 1.2 us)
Sparse Core Ops, SparseCore 0:
  65.1 68.0 reduce-scatter.1
  153.5 35.3 all-gather.1
  195.0 276.6 all-reduce.9
  474.7 162.8 all-reduce.7
where the time goes:
time: 656 us; the launch traced here: 650 us
  waiting for transfers between devices  446 us (68%)
  local copies, waits for them, and re-layouts  118 us (18%)
  starting transfers between devices  48.9 us (7%)
  matrix products  18.3 us (3%)
  between operations  14.1 us (2%)
    psum x1, waiting for transfers between devices, shards(): grad_w1 = lax.psum(local_one, ('slab', 'filt'))  236 us
    psum x1, waiting for transfers between devices, shards(): grad_w2 = lax.psum(local_two, 'slab')  166 us
    unnamed x72, local copies, waits for them, and re-layouts  44.4 us
    concatenate x1, local copies, waits for them, and re-layouts, shards(): jnp.concatenate([wide_cot[1 - a:3 - a + planes_here, 1 - b:3 - b + row_co...  32.1 us
    ppermute x6, starting transfers between devices, padded(): lax.ppermute(lax.slice_in_dim(block, block.shape[dim] - width, None, axis...  28.1 us
    ppermute x6, waiting for transfers between devices, padded(): lax.ppermute(lax.slice_in_dim(block, 0, width, axis=dim), axis, backward)  20.4 us
    slice x2, local copies, waits for them, and re-layouts, shards(): wide_cot[1 - a:3 - a + planes_here, 1 - b:3 - b + row_count, 1 - c:3 - c...  16.4 us
    reduce_scatter x1, waiting for transfers between devices, shards(): lax.psum_scatter(whole_term, 'filt', scatter_dimension=3, tiled=True)  15.7 us
  transfers between devices with their start and end apart: 17, of which 8 were waited for; matrix products, arithmetic and copies ran while one was open for 20% of the time, Pallas kernels for 0%

commit v1 on v0

v1 whole, which is shorter than its diff:
```python
import functools
import math

import jax
import jax.numpy as jnp
from jax import lax
from jax.experimental import pallas as pl
from jax.experimental.pallas import tpu as pltpu
from jax.sharding import PartitionSpec as P

leak_slope = 0.3
bf16 = jnp.bfloat16
f32 = jnp.float32
f16 = jnp.float16
top = 13.0
planes, rows, cols = 2, 16, 64
lanes = planes * cols
voxels = rows * lanes
block = 16
taps = 27

same_core = [[2 * i + core for i in range(8)] for core in range(2)]
core_swap = [(i, i ^ 1) for i in range(16)]
swaps = (2, 4, 12, 1)
block_order = [0]
for swap in swaps:
    block_order += [other ^ swap for other in block_order]
slab_up = [(i, i + 1) for i in range(15)]
slab_down = [(i + 1, i) for i in range(15)]


def params():
    return pltpu.CompilerParams(vmem_limit_bytes=48 * 1024 * 1024)


def cost(flops, moved):
    return pl.CostEstimate(flops=flops, bytes_accessed=moved, transcendentals=0)


def shape(dims, dtype):
    return jax.ShapeDtypeStruct(dims, dtype)


def whole(count):
    return [pl.BlockSpec(memory_space=pltpu.VMEM)] * count


def scalar_spec():
    return pl.BlockSpec(memory_space=pltpu.SMEM)


def exponent(value):
    most = jnp.max(jnp.max(jnp.abs(value), axis=0, keepdims=True), axis=1, keepdims=True)
    return jnp.ceil(jnp.log2(jnp.maximum(most, 2.0**-100)))


def weight_kernel(place, weight, own, sent):
    flat = weight[...].astype(f32).reshape(taps * block, 256).T.astype(bf16)
    low, high = flat[:128], flat[128:]
    own[...] = jnp.where(place[0] == 0, low, high)
    sent[...] = jnp.where(place[0] == 0, high, low)


def pack_kernel(cot, x, low, high):
    for plane, out in ((0, low), (1, high)):
        field = cot[plane].reshape(rows * block, cols)
        piece = x[plane]
        side = jnp.concatenate(
            [piece[:, :cols], piece[:, cols:], jnp.zeros((2 * cols, cols), bf16)], axis=0
        )
        out[...] = jnp.concatenate([field, side], axis=1)


def message_kernel(pre, x, packed, out):
    value = pre[...].astype(f32).reshape(lanes, 256)
    active = jnp.where(value > 0, value, leak_slope * value).astype(bf16)
    own = x[...].reshape(lanes, 128)
    for i in range(8):
        out[i, 0] = active[:, :128]
        out[i, 1] = active[:, 128:]
        out[i, 2] = own


def shifted_rows(field, b):
    gap = jnp.zeros((field.shape[0], lanes), field.dtype)
    if b == 1:
        return jnp.concatenate([gap, field[:, :-lanes]], axis=1)
    if b == -1:
        return jnp.concatenate([field[:, lanes:], gap], axis=1)
    return field


def shifted_columns(field, c):
    if c == 0:
        return field
    width = field.shape[1]
    col = lax.broadcasted_iota(jnp.int32, field.shape, 1) % cols
    edge = 0 if c == 1 else cols - 1
    return jnp.where(col == edge, jnp.zeros_like(field), pltpu.roll(field, c % width, axis=1))


def fill_columns(own, low, high, out):
    below = low[:, :cols].reshape(rows, block, cols)
    above = high[:, :cols].reshape(rows, block, cols)
    parts = [below, own[0], own[1], above]
    for a in (-1, 0, 1):
        pieces = []
        for r in range(rows):
            pieces += [parts[1 - a][r].astype(f32), parts[2 - a][r].astype(f32)]
        field = jnp.concatenate(
            [jnp.concatenate(pieces[2 * r : 2 * r + 2], axis=1) for r in range(rows)], axis=1
        )
        for c in (-1, 0, 1):
            moved = shifted_columns(field, c).astype(bf16)
            for b in (-1, 0, 1):
                tap = 9 * (a + 1) + 3 * (b + 1) + c + 1
                out[tap * block : (tap + 1) * block, :] = shifted_rows(moved, b)


def back_kernel(own, other, own_low, own_high, other_low, other_high, own_w, other_w, out, cot_cols, other_cols):
    fill_columns(own, own_low, own_high, cot_cols)
    fill_columns(other, other_low, other_high, other_cols)
    total = jnp.dot(own_w[...], cot_cols[...], preferred_element_type=f32)
    total += jnp.dot(other_w[...], other_cols[...], preferred_element_type=f32)
    power = exponent(total)
    out[:, :, :voxels] = (total * jnp.exp2(top - power)).reshape(8, block, voxels)
    rims = [
        jnp.concatenate([pack[0:cols, cols:], pack[cols : 2 * cols, cols:]], axis=1)
        for pack in (own_low, own_high)
    ]
    rim = jnp.concatenate(rims, axis=0).astype(f32)
    rim_power = exponent(rim)
    rim = rim * jnp.exp2(top - rim_power)
    side = [
        jnp.broadcast_to(power, (block, cols)),
        jnp.broadcast_to(rim_power, (block, cols)),
    ] + [rim[g * block : (g + 1) * block] for g in range(8)]
    side = jnp.concatenate(side, axis=1)
    for i in range(8):
        out[i, :, voxels:] = side


def second_kernel(place, cot_cols, own, other, grad, slope, active):
    core = place[0]
    first = place[0] * 128 + place[1] // 2 * block
    for i in range(8):
        for part, side in ((own, core), (other, 1 - core)):
            here = pl.ds(pl.multiple_of((2 * i + side) * lanes, lanes), lanes)
            active[here, 0:128] = part[i, 0]
            active[here, 128:256] = part[i, 1]
    grad[...] = jnp.dot(cot_cols[...], active[...], preferred_element_type=f32)
    positive = jnp.where(active[...].astype(f32) > 0, 1.0, 0.0).astype(bf16)
    mid = lax.broadcasted_iota(jnp.int32, (block, 256), 1)
    row = lax.broadcasted_iota(jnp.int32, (block, 256), 0)
    pick = jnp.where(mid == row + first, 1.0, 0.0).astype(bf16)
    mask = lax.dot_general(pick, positive, (((1,), (1,)), ((), ())), preferred_element_type=f32)
    slope[...] = jnp.where(mask > 0.5, 1.0, leak_slope)


def inputs_kernel(place, own, other, own_rims, other_rims, inputs):
    core = place[0]
    for i in range(8):
        for part, rims, at, side in ((own, own_rims, voxels, core), (other, other_rims, 0, 1 - core)):
            here = pl.ds(pl.multiple_of((2 * i + side) * lanes, lanes), lanes)
            middle = part[i, 2]
            scale = jnp.exp2(rims[i, 0:1, at + cols : at + cols + 1] - top)
            at += 128
            rim = [rims[i, :, at + g * 128 : at + (g + 1) * 128] for g in range(8)]
            rim = (jnp.concatenate(rim, axis=0) * scale).astype(bf16)
            inputs[here, 0:128] = jnp.concatenate([rim[:cols], middle[:cols]], axis=0)
            inputs[here, 128:256] = middle
            inputs[here, 256:384] = jnp.concatenate([middle[cols:], rim[cols:]], axis=0)


def split(value):
    high = value.astype(bf16)
    return high, (value - high.astype(f32)).astype(bf16)


def first_kernel(parts, slope, inputs, second, out, error, shifted):
    total = jnp.zeros((block, voxels), f32)
    for i in range(8):
        total = total + parts[i, :, :voxels] * jnp.exp2(parts[i, :, voxels : voxels + 1] - top)
    total = total * slope[...]
    error_power = exponent(total)
    error[:, :voxels] = total * jnp.exp2(top - error_power)
    error[:, voxels:] = jnp.broadcast_to(error_power, (block, 128))
    for c in (-1, 0, 1):
        pair = split(shifted_columns(total, c))
        for b in (-1, 0, 1):
            at = (3 * (b + 1) + c + 1) * 2 * block
            for k in range(2):
                shifted[at + k * block : at + (k + 1) * block, :] = shifted_rows(pair[k], b)
    grad = jnp.dot(shifted[...], inputs[...], preferred_element_type=f32)
    grad = grad.reshape(9, 2, block, 384)
    grad = grad[:, 0] + grad[:, 1]
    power = exponent(grad.reshape(9 * block, 384))
    grad = grad * jnp.exp2(top - power).reshape(1, 1, 1)
    for a in range(3):
        for bc in range(9):
            tap = 9 * a + bc
            out[tap * block : (tap + 1) * block, 0:128] = grad[bc, :, a * 128 : (a + 1) * 128]
    second_power = exponent(second[...])
    out[0 : taps * block, 128:384] = second[...] * jnp.exp2(top - second_power)
    out[taps * block :, 0:384] = jnp.zeros((5 * block, 384), f32)
    out[:, 384:448] = jnp.broadcast_to(power, (32 * block, cols))
    out[:, 448:512] = jnp.broadcast_to(second_power, (32 * block, cols))


def sum_kernel(place, sums, out, second_power):
    power = jnp.max(sums[:, :, 384:512], axis=0)
    low, high = power[:, 0:1], power[:, cols : cols + 1]
    first = jnp.zeros((2 * block, 128), f32)
    second = jnp.zeros((2 * block, 256), f32)
    for i in range(16):
        first += sums[i, :, 0:128] * jnp.exp2(sums[i, :, 384:385] - low - 4.0)
        second += sums[i, :, 128:384] * jnp.exp2(sums[i, :, 448:449] - high - 4.0)
    row = lax.broadcasted_iota(jnp.int32, (2 * block, 128), 0)
    keep = jnp.logical_or(place[2] != 13, row < block)
    out[:, 0:128] = jnp.where(keep, first, low + 4.0)
    out[:, 128:384] = second
    second_power[...] = jnp.broadcast_to(high[0:8] + 4.0, (8, 128))


def second_scale_kernel(grad_scale, grad, power, out):
    scale = jnp.exp2(power[0:1, 0:1] - top) * grad_scale
    out[...] = grad[...] * scale.reshape(1, 1, 1)


def input_kernel(place, blocks, weight, middle, to_low, to_high, field):
    filt = place[1]
    for j, other in enumerate(block_order):
        source = filt ^ other
        here = pl.ds(pl.multiple_of((source % 2 * 8 + source // 2) * block, block), block)
        scale = jnp.exp2(blocks[j, 0:1, voxels : voxels + 1] - top)
        for b in range(3):
            row = filt + b - 1
            at = pl.multiple_of(jnp.clip(row, 0, rows - 1) * lanes, lanes)
            inside = jnp.logical_and(row >= 0, row < rows)
            piece = jnp.where(inside, blocks[j, :, pl.ds(at, lanes)] * scale, 0.0)
            field[here, b * lanes : (b + 1) * lanes] = piece
    field = field[...]
    total = jnp.zeros((3 * 128, 2 * lanes), f32)
    for c in (-1, 0, 1):
        pair = split(shifted_columns(field, c))
        for b in (-1, 0, 1):
            at = (1 - b) * lanes
            window = jnp.concatenate([half[:, at : at + lanes] for half in pair], axis=1)
            tap = 3 * (b + 1) + c + 1
            taken = jnp.concatenate([weight[9 * a + tap] for a in range(3)], axis=0)
            total += jnp.dot(taken, window, preferred_element_type=f32)
    total = (total[:, :lanes] + total[:, lanes:]).T
    back, here, ahead = total[:, :128], total[:, 128:256], total[:, 256:]
    to_low[...] = back[:cols]
    to_high[...] = ahead[cols:]
    middle[0:cols] = here[:cols] + back[cols:]
    middle[cols:] = here[cols:] + ahead[:cols]


def rim_kernel(middle, low, high, out):
    out[0:cols] = (middle[0:cols] + low[...]).astype(bf16)
    out[cols:] = (middle[cols:] + high[...]).astype(bf16)


def gather_kernel(grad_scale, place, part, power, *rest):
    out = rest[-1]
    scale = jnp.exp2(power[...].reshape(128, 128) - top) * grad_scale
    row = lax.broadcasted_iota(jnp.int32, (128, 256), 0)
    lane = lax.broadcasted_iota(jnp.int32, (128, 256), 1) % 128
    unit = jnp.where(row == lane, 1.0, 0.0).astype(bf16)
    for t in range(9):
        value = part[:, t * block : (t + 1) * block].reshape(128, 128) * scale
        out[t] = lax.dot_general(
            unit,
            jnp.concatenate(split(value), axis=1),
            (((1,), (1,)), ((), ())),
            preferred_element_type=f32,
        )


def gather(grad_scale, place, wide, swapped, result):
    def half(i, place):
        return (i, 0, 1 - place[0] if swapped else place[0])

    extra = [] if result is None else [result]
    return pl.pallas_call(
        functools.partial(gather_kernel, grad_scale),
        out_shape=shape((taps, 128, 256), f32),
        grid_spec=pltpu.PrefetchScalarGridSpec(
            num_scalar_prefetch=1,
            grid=(3,),
            in_specs=[
                pl.BlockSpec((8, 9 * block, 128), lambda i, place: (0, i, 0)),
                pl.BlockSpec((8, block, 128), lambda i, place: (0, taps, 0)),
            ]
            + [pl.BlockSpec(memory_space=pl.ANY)] * len(extra),
            out_specs=pl.BlockSpec((9, 128, 128), half),
        ),
        input_output_aliases={3: 0} if extra else {},
        compiler_params=params(),
        cost_estimate=cost(2 * 128 * 128 * 256 * taps, 4 << 20),
        name="gather_other" if swapped else "gather_own",
    )(place, wide, wide, *extra)


def shards(cotangent, pre_act, layer_input, weight_one, weight_two):
    grad_scale = 1.0 / math.sqrt(voxels * 16)
    filt = lax.axis_index("filt")
    core = filt % 2
    place = jnp.stack([core, filt, lax.axis_index("slab")]).astype(jnp.int32)

    cot = cotangent.transpose(0, 1, 3, 2)
    x = layer_input.reshape(planes, cols, 128)
    pre = pre_act.reshape(planes, cols, 256)
    to_low, to_high = pl.pallas_call(
        pack_kernel,
        out_shape=[shape((256, 128), bf16)] * 2,
        in_specs=whole(2),
        out_specs=whole(2),
        compiler_params=params(),
        name="pack",
    )(cot, x)
    low = lax.ppermute(to_high, "slab", slab_up)
    high = lax.ppermute(to_low, "slab", slab_down)
    message = pl.pallas_call(
        message_kernel,
        out_shape=shape((8, 3, 128, 128), bf16),
        in_specs=whole(2) + [pl.BlockSpec(memory_space=pl.ANY)],
        out_specs=whole(1)[0],
        compiler_params=params(),
        name="message",
    )(pre, x, to_low)
    own_rows = lax.all_to_all(
        message, "filt", split_axis=0, concat_axis=0, tiled=True, axis_index_groups=same_core
    )
    other = lax.ppermute(cot, "filt", core_swap)
    own_w, sent_w = pl.pallas_call(
        weight_kernel,
        out_shape=[shape((128, taps * block), bf16)] * 2,
        in_specs=[scalar_spec()] + whole(1),
        out_specs=whole(2),
        compiler_params=params(),
        name="weights",
    )(place, weight_two.transpose(0, 2, 1))
    other_w = lax.ppermute(sent_w, "filt", core_swap)
    other_low = lax.ppermute(low, "filt", core_swap)
    other_high = lax.ppermute(high, "filt", core_swap)

    partial, cot_cols = pl.pallas_call(
        back_kernel,
        out_shape=[shape((8, block, voxels + 1152), f32), shape((taps * block, voxels), bf16)],
        in_specs=whole(8),
        out_specs=whole(2),
        scratch_shapes=[pltpu.VMEM((taps * block, voxels), bf16)],
        compiler_params=params(),
        cost_estimate=cost(2 * 864 * 128 * 2048, 4 << 20),
        name="back",
    )(cot, other, low, high, other_low, other_high, own_w, other_w)
    partial = partial.astype(f16)
    own_rows, _ = lax.optimization_barrier((own_rows, partial))
    parts = lax.all_to_all(
        partial, "filt", split_axis=0, concat_axis=0, tiled=True, axis_index_groups=same_core
    )
    other_rows = lax.ppermute(own_rows, "filt", core_swap)
    second, slope = pl.pallas_call(
        second_kernel,
        out_shape=[shape((taps * block, 256), f32), shape((block, voxels), f32)],
        in_specs=[scalar_spec()] + whole(3),
        out_specs=whole(2),
        scratch_shapes=[pltpu.VMEM((voxels, 256), bf16)],
        compiler_params=params(),
        cost_estimate=cost(2 * 432 * 2048 * 256, 6 << 20),
        name="second",
    )(place, cot_cols, own_rows, other_rows)
    parts, _ = lax.optimization_barrier((parts, second))
    other_rims = lax.ppermute(parts[:, :, voxels:], "filt", core_swap).astype(f32)
    parts = parts.astype(f32)
    inputs = pl.pallas_call(
        inputs_kernel,
        out_shape=shape((voxels, 384), bf16),
        in_specs=[scalar_spec()] + whole(4),
        out_specs=whole(1)[0],
        compiler_params=params(),
        name="inputs",
    )(place, own_rows, other_rows, parts, other_rims)

    merged, error = pl.pallas_call(
        first_kernel,
        out_shape=[shape((512, 512), f32), shape((block, voxels + 128), f32)],
        in_specs=whole(4),
        out_specs=whole(2),
        scratch_shapes=[pltpu.VMEM((18 * block, voxels), bf16)],
        compiler_params=params(),
        cost_estimate=cost(2 * 288 * 2048 * 384, 6 << 20),
        name="first",
    )(parts, slope, inputs, second)

    sums = lax.all_to_all(
        merged.reshape(16, 32, 512).astype(f16), "slab", split_axis=0, concat_axis=0, tiled=True
    )
    blocks = error.astype(f16)[None]
    steps = []
    for swap in swaps:
        arrived = lax.ppermute(blocks, "filt", [(i, i ^ swap) for i in range(16)])
        blocks = jnp.concatenate([blocks, arrived], axis=0)
        steps.append(blocks)
    middle, rim_low, rim_high = pl.pallas_call(
        input_kernel,
        out_shape=[shape((lanes, 128), f32)] + [shape((cols, 128), f32)] * 2,
        in_specs=[scalar_spec()] + whole(2),
        out_specs=whole(3),
        scratch_shapes=[pltpu.VMEM((256, 3 * lanes), f32)],
        compiler_params=params(),
        cost_estimate=cost(2 * 128 * 256 * 256 * taps, 4 << 20),
        name="input",
    )(place, blocks.astype(f32), weight_one)
    rim_low, rim_high = (
        lax.ppermute(rim_high, "slab", slab_up),
        lax.ppermute(rim_low, "slab", slab_down),
    )
    grad_x0 = pl.pallas_call(
        rim_kernel,
        out_shape=shape((lanes, 128), bf16),
        in_specs=whole(3),
        out_specs=whole(1)[0],
        compiler_params=params(),
        name="rim",
    )(middle, rim_low, rim_high).reshape(planes, 1, cols, 128)
    sums, _ = lax.optimization_barrier((sums, steps[1]))
    mine, second_power = pl.pallas_call(
        sum_kernel,
        out_shape=[shape((32, 384), f32), shape((8, 128), f32)],
        in_specs=[scalar_spec()] + whole(1),
        out_specs=whole(2),
        compiler_params=params(),
        name="sum",
    )(place, sums.astype(f32))
    near = jnp.broadcast_to(mine.astype(f16)[None], (16, 32, 384))
    near = lax.all_to_all(near, "slab", split_axis=0, concat_axis=0, tiled=True)
    near, _ = lax.optimization_barrier((near, middle))
    near = near.reshape(32, block, 384)
    wide = jnp.broadcast_to(near[None, :28, :, :128], (8, 28, block, 128))
    wide = wide.reshape(8, 28 * block, 128)
    wide = lax.all_to_all(
        wide, "filt", split_axis=0, concat_axis=0, tiled=True, axis_index_groups=same_core
    )
    grad_w2 = pl.pallas_call(
        functools.partial(second_scale_kernel, grad_scale),
        out_shape=shape((taps, block, 256), f32),
        in_specs=whole(2),
        out_specs=whole(1)[0],
        compiler_params=params(),
        name="second_scale",
    )(near[:taps, :, 128:].astype(f32), second_power).transpose(0, 2, 1)
    wide, grad_w2, grad_x0 = lax.optimization_barrier((wide, grad_w2, grad_x0))
    other_wide = lax.ppermute(wide, "filt", core_swap)
    grad_w1 = gather(grad_scale, place, wide.astype(f32), False, None)
    grad_w1 = gather(grad_scale, place, other_wide.astype(f32), True, grad_w1)
    return (grad_w2, grad_w1, grad_x0)


def solution(mesh):
    return jax.shard_map(
        shards,
        mesh=mesh,
        in_specs=(
            P("slab", None, None, "filt"),
            P("slab", "filt", None, None),
            P("slab", "filt", None, None),
            P(),
            P(None, None, "filt"),
        ),
        out_specs=(P(None, None, "filt"), P(), P("slab", "filt", None, None)),
        check_vma=False,
    )
```

time: 656 us -> 133 us (0.20)
  the two profiles are of different devices: /device:TPU:2 before, /device:TPU:1 now
where the time goes in v1:
time: 133 us; the launch traced here: 132 us
  starting transfers between devices  59.2 us (45%)
  waiting for transfers between devices  40.8 us (31%)
  Pallas kernels  17 us (13%)
  local copies, waits for them, and re-layouts  9.66 us (7%)
  other arithmetic  4.08 us (3%)
    all_to_all x1, starting transfers between devices, shards(): lax.all_to_all(partial, 'filt', split_axis=0, concat_axis=0, tiled=True,...  9.91 us
    ppermute x4, waiting for transfers between devices, shards(): arrived = lax.ppermute(blocks, 'filt', [(i, i ^ swap) for i in range(16)])  9.34 us
    all_to_all x1, waiting for transfers between devices, shards(): near = lax.all_to_all(near, 'slab', split_axis=0, concat_axis=0, tiled=True)  9.04 us
    all_to_all x1, starting transfers between devices, shards(): lax.all_to_all(merged.reshape(16, 32, 512).astype(f16), 'slab', split_axi...  8.22 us
    all_to_all x1, waiting for transfers between devices, shards(): lax.all_to_all(partial, 'filt', split_axis=0, concat_axis=0, tiled=True,...  7.58 us
    all_to_all x1, starting transfers between devices, shards(): lax.all_to_all(message, 'filt', split_axis=0, concat_axis=0, tiled=True,...  6.33 us
    pallas_call x2, Pallas kernels, gather(): pl.pallas_call(functools.partial(gather_kernel, grad_scale), out_shape=sh...  6.05 us
    unnamed x21, local copies, waits for them, and re-layouts  5.63 us
  transfers between devices with their start and end apart: 20, of which 12 were waited for; matrix products, arithmetic and copies ran while one was open for 5% of the time, Pallas kernels for 8%

profile of v1, /device:TPU:1, one launch (start us, length us, event | category | flops | bytes accessed | tf_op | source)
XLA Modules:
  0.0 131.7 jit_solution(663825477106796339)
XLA Ops:
  5.0 6.3 %all-to-all-start.1 = ((bf16[8,3,128,128]{3,2,1,0:T(8,128)(2,1)}), bf16[8,3,128,128]{3,2,1,0:T(8,128)(2,1)S(1)}, u32[]{:S(2)}, u32[]{:S(2)}) async-start(bf16[8,3,128,128]{3,2,1,0:T(8,128)(2,1)} %message.1), calls=%async_computation.1 | async-start | bytes 1572864 | tf_op jit(solution)/shard_map/all_to_all | solution.py:333
  12.6 5.5 %collective-permute-start.1 = (bf16[256,128]{1,0:T(8,128)(2,1)S(1)}, bf16[256,128]{1,0:T(8,128)(2,1)S(1)}, u32[]{:S(2)}, u32[]{:S(2)}) collective-permute-start(bf16[256,128]{1,0:T(8,128)(2,1)S(1)} %get-tuple-element.25), channel_id=1, source_target_pairs={{0,16},{16,32},{32,48},{48,64},{64,80},{80,96},{96,112},{112,128},... | collective-permute-start | bytes 196616 | tf_op jit(solution)/shard_map/ppermute | solution.py:323
  20.7 1.5 %collective-permute-start.3 = (bf16[256,128]{1,0:T(8,128)(2,1)S(1)}, bf16[256,128]{1,0:T(8,128)(2,1)S(1)}, u32[]{:S(2)}, u32[]{:S(2)}) collective-permute-start(bf16[256,128]{1,0:T(8,128)(2,1)S(1)} %collective-permute-done.1.own_low), channel_id=1, source_target_pairs={{0,1},{1,0},{2,3},{3,2},{4,5},{5,4},{6,7},{7,6},{8,9},{9,8},{10,11... | collective-permute-start | bytes 196616 | tf_op jit(solution)/shard_map/ppermute | solution.py:346
  23.6 1.6 %back.1 = (f32[8,16,3200]{2,1,0:T(8,128)S(1)}, bf16[432,2048]{1,0:T(8,128)(2,1)S(1)}) custom-call(bf16[2,16,16,64]{3,2,1,0:T(8,128)(2,1)S(1)} %bitcast.19, bf16[2,16,16,64]{3,2,1,0:T(8,128)(2,1)S(1)} %collective-permute-done.other, bf16[256,128]{1,0:T(8,128)(2,1)S(1)} %collective-permute-done.1.own_low, ...), custom_call_target="tpu_custom_call" | custom-call | flops 452984832 | bytes 4194304 | tf_op jit(solution)/shard_map/back/pallas_call | solution.py:349
  26.2 9.9 %all-to-all-start = ((f16[8,16,3200]{2,1,0:T(8,128)(2,1)}), f16[8,16,3200]{2,1,0:T(8,128)(2,1)}, u32[]{:S(2)}, u32[]{:S(2)}) async-start(f16[8,16,3200]{2,1,0:T(8,128)(2,1)} %convert_element_type.36), calls=%async_computation | async-start | bytes 1638400 | tf_op jit(solution)/shard_map/all_to_all | solution.py:361
  36.7 1.9 %collective-permute-done.6.other = bf16[8,3,128,128]{3,2,1,0:T(8,128)(2,1)S(1)} collective-permute-done((bf16[8,3,128,128]{3,2,1,0:T(8,128)(2,1)S(1)}, bf16[8,3,128,128]{3,2,1,0:T(8,128)(2,1)S(1)}, u32[]{:S(2)}, u32[]{:S(2)}) %collective-permute-start.6) | collective-permute-done | bytes 786464 | tf_op jit(solution)/shard_map/ppermute | solution.py:364
  38.6 1.6 %second.1 = (f32[432,256]{1,0:T(8,128)S(1)}, f32[16,2048]{1,0:T(8,128)S(1)}) custom-call(s32[3]{0:T(128)S(1)} %pad_add_fusion.place, bf16[432,2048]{1,0:T(8,128)(2,1)S(1)} %get-tuple-element.30.cot_cols, bf16[8,3,128,128]{3,2,1,0:T(8,128)(2,1)S(1)} %all-to-all-done.1.own, bf16[8,3,128,128]{3,2,1,0:T(8,128)(2,1)S(1)} %collective-permute-done.6.other), custom_call_target="tpu_custom_call" | custom-call | flops 452984832 | bytes 6291456 | tf_op jit(solution)/shard_map/second/pallas_call | solution.py:365
  41.0 7.6 %all-to-all-done = f16[8,16,3200]{2,1,0:T(8,128)(2,1)} async-done(((f16[8,16,3200]{2,1,0:T(8,128)(2,1)}), f16[8,16,3200]{2,1,0:T(8,128)(2,1)}, u32[]{:S(2)}, u32[]{:S(2)}) %all-to-all-start) | async-done | bytes 819232 | tf_op jit(solution)/shard_map/all_to_all | solution.py:361
  49.6 1.9 %collective-permute-start.7 = (f16[8,16,1152]{2,1,0:T(8,128)(2,1)S(1)}, f16[8,16,1152]{2,1,0:T(8,128)(2,1)S(1)}, u32[]{:S(2)}, u32[]{:S(2)}) collective-permute-start(f16[8,16,1152]{2,1,0:T(8,128)(2,1)S(1)} %slice.9), channel_id=1, source_target_pairs={{0,1},{1,0},{2,3},{3,2},{4,5},{5,4},{6,7},{7,6},{8,9},{9,8},{10,11... | collective-permute-start | bytes 884744 | tf_op jit(solution)/shard_map/ppermute | solution.py:376
  53.8 1.3 %first.1 = (f32[512,512]{1,0:T(8,128)S(1)}, f32[16,2176]{1,0:T(8,128)S(1)}) custom-call(f32[8,16,3200]{2,1,0:T(8,128)S(1)} %convert_element_type.37.own_rims.parts, f32[16,2048]{1,0:T(8,128)S(1)} %get-tuple-element.34.slope, bf16[2048,384]{1,0:T(8,128)(2,1)S(1)} %inputs.1, f32[432,256]{1,0:T(8,128)S(1)} %copy-done.2), custom_call_target="tpu_custom_call" | custom-call | flops 452984832 | bytes 6291456 | tf_op jit(solution)/shard_map/first/pallas_call | solution.py:387
  55.8 2.6 %collective-permute-done.8 = f16[1,16,2176]{2,1,0:T(8,128)(2,1)S(1)} collective-permute-done((f16[1,16,2176]{2,1,0:T(8,128)(2,1)S(1)}, f16[1,16,2176]{2,1,0:T(8,128)(2,1)S(1)}, u32[]{:S(2)}, u32[]{:S(2)}) %collective-permute-start.8) | collective-permute-done | bytes 69664 | tf_op jit(solution)/shard_map/ppermute | solution.py:404
  59.4 8.2 %all-to-all-start.2 = ((f16[16,32,512]{2,1,0:T(8,128)(2,1)}), f16[16,32,512]{2,1,0:T(8,128)(2,1)S(1)}, u32[]{:S(2)}, u32[]{:S(2)}) async-start(f16[16,32,512]{2,1,0:T(8,128)(2,1)} %bitcast.7), calls=%async_computation.2 | async-start | bytes 1048576 | tf_op jit(solution)/shard_map/all_to_all | solution.py:398
  68.7 6.8 %collective-permute-done.10 = f16[4,16,2176]{2,1,0:T(8,128)(2,1)S(1)} collective-permute-done((f16[4,16,2176]{2,1,0:T(8,128)(2,1)S(1)}, f16[4,16,2176]{2,1,0:T(8,128)(2,1)S(1)}, u32[]{:S(2)}, u32[]{:S(2)}) %collective-permute-start.10) | collective-permute-done | bytes 278560 | tf_op jit(solution)/shard_map/ppermute | solution.py:404
  75.6 2.8 %collective-permute-start.11 = (f16[8,16,2176]{2,1,0:T(8,128)(2,1)S(1)}, f16[8,16,2176]{2,1,0:T(8,128)(2,1)}, u32[]{:S(2)}, u32[]{:S(2)}) collective-permute-start(f16[8,16,2176]{2,1,0:T(8,128)(2,1)S(1)} %pad_maximum_fusion), channel_id=1, source_target_pairs={{0,1},{1,0},{2,3},{3,2},{4,5},{5,4},{6,7},{7,6},{8,9},{9,8},{10,11... | collective-permute-start | bytes 1671176 | tf_op jit(solution)/shard_map/ppermute | solution.py:404
  78.4 5.6 %all-to-all-done.2 = f16[16,32,512]{2,1,0:T(8,128)(2,1)S(1)} async-done(((f16[16,32,512]{2,1,0:T(8,128)(2,1)}), f16[16,32,512]{2,1,0:T(8,128)(2,1)S(1)}, u32[]{:S(2)}, u32[]{:S(2)}) %all-to-all-start.2) | async-done | bytes 524320 | tf_op jit(solution)/shard_map/all_to_all | solution.py:398
  85.8 3.7 %all-to-all-start.3 = ((f16[16,32,384]{2,1,0:T(8,128)(2,1)}), f16[16,32,384]{2,1,0:T(8,128)(2,1)S(1)}, u32[]{:S(2)}, u32[]{:S(2)}) async-start(f16[16,32,384]{2,1,0:T(8,128)(2,1)} %broadcast_in_dim.18), calls=%async_computation.3 | async-start | bytes 786432 | tf_op jit(solution)/shard_map/all_to_all | solution.py:439
  92.3 1.5 %input.1 = (f32[128,128]{1,0:T(8,128)S(1)}, f32[64,128]{1,0:T(8,128)S(1)}, f32[64,128]{1,0:T(8,128)S(1)}) custom-call(s32[3]{0:T(128)S(1)} %pad_add_fusion.place, f32[16,16,2176]{2,1,0:T(8,128)S(1)} %convert_element_type.44.blocks, bf16[27,128,256]{2,1,0:T(8,128)(2,1)S(1)} %copy-done), custom_call_target="tpu_custom_call" | custom-call | flops 452984832 | bytes 4194304 | tf_op jit(solution)/shard_map/input/pallas_call | solution.py:407
  93.8 9.0 %all-to-all-done.3 = f16[16,32,384]{2,1,0:T(8,128)(2,1)S(1)} async-done(((f16[16,32,384]{2,1,0:T(8,128)(2,1)}), f16[16,32,384]{2,1,0:T(8,128)(2,1)S(1)}, u32[]{:S(2)}, u32[]{:S(2)}) %all-to-all-start.3) | async-done | bytes 393248 | tf_op jit(solution)/shard_map/all_to_all | solution.py:439
  103.9 5.5 %all-to-all-start.4 = ((f16[8,448,128]{2,1,0:T(8,128)(2,1)}), f16[8,448,128]{2,1,0:T(8,128)(2,1)S(1)}, u32[]{:S(2)}, u32[]{:S(2)}) async-start(f16[8,448,128]{2,1,0:T(8,128)(2,1)} %broadcast_in_dim.20), calls=%async_computation.4 | async-start | bytes 1835008 | tf_op jit(solution)/shard_map/all_to_all | solution.py:444
  109.4 2.9 %collective-permute-start.12 = (f32[64,128]{1,0:T(8,128)S(1)}, f32[64,128]{1,0:T(8,128)S(1)}, u32[]{:S(2)}, u32[]{:S(2)}) collective-permute-start(f32[64,128]{1,0:T(8,128)S(1)} %get-tuple-element.42), channel_id=1, source_target_pairs={{0,16},{16,32},{32,48},{48,64},{64,80},{80,96},{96,112},{112,128},... | collective-permute-start | bytes 98312 | tf_op jit(solution)/shard_map/ppermute | solution.py:418
  113.6 4.1 %collective-permute-done.12.low = f32[64,128]{1,0:T(8,128)S(1)} collective-permute-done((f32[64,128]{1,0:T(8,128)S(1)}, f32[64,128]{1,0:T(8,128)S(1)}, u32[]{:S(2)}, u32[]{:S(2)}) %collective-permute-start.12) | collective-permute-done | bytes 32800 | tf_op jit(solution)/shard_map/ppermute | solution.py:418
  120.9 4.5 %collective-permute-start.14 = (f16[8,448,128]{2,1,0:T(8,128)(2,1)S(1)}, f16[8,448,128]{2,1,0:T(8,128)(2,1)S(1)}, u32[]{:S(2)}, u32[]{:S(2)}) collective-permute-start(f16[8,448,128]{2,1,0:T(8,128)(2,1)S(1)} %all-to-all-done.4), channel_id=1, source_target_pairs={{0,1},{1,0},{2,3},{3,2},{4,5},{5,4},{6,7},{7,6},{8,9},{9,8},{10,11... | collective-permute-start | bytes 2752520 | tf_op jit(solution)/shard_map/ppermute | solution.py:456
  125.5 3.0 %gather_own.1.rest_0_ = f32[27,128,256]{2,1,0:T(8,128)} custom-call(s32[3]{0:T(128)S(1)} %pad_add_fusion.place, f32[8,448,128]{2,1,0:T(8,128)S(1)} %convert_element_type.47.part.power, f32[8,448,128]{2,1,0:T(8,128)S(1)} %convert_element_type.47.part.power), custom_call_target="tpu_custom_call" | custom-call | flops 226492416 | bytes 4194304 | tf_op jit(solution)/shard_map/gather_own/pallas_call | solution.py:286
  128.7 3.0 %gather_other.1 = f32[27,128,256]{2,1,0:T(8,128)} custom-call(s32[3]{0:T(128)S(1)} %pad_add_fusion.place, f32[8,448,128]{2,1,0:T(8,128)S(1)} %convert_element_type.46.part.power, f32[8,448,128]{2,1,0:T(8,128)S(1)} %convert_element_type.46.part.power, f32[27,128,256]{2,1,0:T(8,128)} %gather_own.1.rest_0_), custom_call_target="tpu_custom_call", output_to_operand_aliasing={{}: (3, {})} | custom-call | flops 226492416 | bytes 4194304 | tf_op jit(solution)/shard_map/gather_other/pallas_call | solution.py:286
  (70 shorter events, 28.3 us)
Async XLA Ops:
  4.0 14.2 %copy-start.3 = (bf16[27,256,16]{1,2,0:T(8,128)(2,1)S(1)}, bf16[27,256,16]{1,2,0:T(8,128)(2,1)}, u32[]{:S(2)}) copy-start(bf16[27,256,16]{1,2,0:T(8,128)(2,1)} %param.9) | copy-start | bytes 663556
  5.0 15.3 %copy-start.5 = (bf16[2,16,64,16]{2,3,1,0:T(8,128)(2,1)S(1)}, bf16[2,16,64,16]{2,3,1,0:T(8,128)(2,1)}, u32[]{:S(2)}) copy-start(bf16[2,16,64,16]{2,3,1,0:T(8,128)(2,1)} %param.5) | copy-start | bytes 196612
  5.0 21.1 %all-to-all-start.1 = ((bf16[8,3,128,128]{3,2,1,0:T(8,128)(2,1)}), bf16[8,3,128,128]{3,2,1,0:T(8,128)(2,1)S(1)}, u32[]{:S(2)}, u32[]{:S(2)}) async-start(bf16[8,3,128,128]{3,2,1,0:T(8,128)(2,1)} %message.1), calls=%async_computation.1 | async-start | bytes 1572864 | tf_op jit(solution)/shard_map/all_to_all | solution.py:333
  11.4 10.9 %collective-permute-start.2 = (bf16[256,128]{1,0:T(8,128)(2,1)S(1)}, bf16[256,128]{1,0:T(8,128)(2,1)S(1)}, u32[]{:S(2)}, u32[]{:S(2)}) collective-permute-start(bf16[256,128]{1,0:T(8,128)(2,1)S(1)} %get-tuple-element.26.packed), channel_id=1, source_target_pairs={{16,0},{32,16},{48,32},{64,48},{80,64},{96,80},{112,96},{128,112},... | collective-permute-start | bytes 196616 | tf_op jit(solution)/shard_map/ppermute | solution.py:324
  12.6 8.1 %collective-permute-start.1 = (bf16[256,128]{1,0:T(8,128)(2,1)S(1)}, bf16[256,128]{1,0:T(8,128)(2,1)S(1)}, u32[]{:S(2)}, u32[]{:S(2)}) collective-permute-start(bf16[256,128]{1,0:T(8,128)(2,1)S(1)} %get-tuple-element.25), channel_id=1, source_target_pairs={{0,16},{16,32},{32,48},{48,64},{64,80},{80,96},{96,112},{112,128},... | collective-permute-start | bytes 196616 | tf_op jit(solution)/shard_map/ppermute | solution.py:323
  19.0 3.4 %collective-permute-start.5 = (bf16[128,432]{1,0:T(8,128)(2,1)S(1)}, bf16[128,432]{1,0:T(8,128)(2,1)S(1)}, u32[]{:S(2)}, u32[]{:S(2)}) collective-permute-start(bf16[128,432]{1,0:T(8,128)(2,1)S(1)} %get-tuple-element.28), channel_id=1, source_target_pairs={{0,1},{1,0},{2,3},{3,2},{4,5},{5,4},{6,7},{7,6},{8,9},{9,8},{10,11... | collective-permute-start | bytes 331784 | tf_op jit(solution)/shard_map/ppermute | solution.py:345
  20.3 2.0 %collective-permute-start = (bf16[2,16,16,64]{3,2,1,0:T(8,128)(2,1)S(1)}, bf16[2,16,16,64]{3,2,1,0:T(8,128)(2,1)S(1)}, u32[]{:S(2)}, u32[]{:S(2)}) collective-permute-start(bf16[2,16,16,64]{3,2,1,0:T(8,128)(2,1)S(1)} %bitcast.18), channel_id=1, source_target_pairs={{0,1},{1,0},{2,3},{3,2},{4,5},{5,4},{6,7},{7,6},{8,9},{9,8},{10,11... | collective-permute-start | bytes 196616 | tf_op jit(solution)/shard_map/ppermute | solution.py:336
  20.7 2.4 %collective-permute-start.3 = (bf16[256,128]{1,0:T(8,128)(2,1)S(1)}, bf16[256,128]{1,0:T(8,128)(2,1)S(1)}, u32[]{:S(2)}, u32[]{:S(2)}) collective-permute-start(bf16[256,128]{1,0:T(8,128)(2,1)S(1)} %collective-permute-done.1.own_low), channel_id=1, source_target_pairs={{0,1},{1,0},{2,3},{3,2},{4,5},{5,4},{6,7},{7,6},{8,9},{9,8},{10,11... | collective-permute-start | bytes 196616 | tf_op jit(solution)/shard_map/ppermute | solution.py:346
  22.3 1.3 collective-permute-start.4
  26.2 22.4 %all-to-all-start = ((f16[8,16,3200]{2,1,0:T(8,128)(2,1)}), f16[8,16,3200]{2,1,0:T(8,128)(2,1)}, u32[]{:S(2)}, u32[]{:S(2)}) async-start(f16[8,16,3200]{2,1,0:T(8,128)(2,1)} %convert_element_type.36), calls=%async_computation | async-start | bytes 1638400 | tf_op jit(solution)/shard_map/all_to_all | solution.py:361
  36.1 2.5 %collective-permute-start.6 = (bf16[8,3,128,128]{3,2,1,0:T(8,128)(2,1)S(1)}, bf16[8,3,128,128]{3,2,1,0:T(8,128)(2,1)S(1)}, u32[]{:S(2)}, u32[]{:S(2)}) collective-permute-start(bf16[8,3,128,128]{3,2,1,0:T(8,128)(2,1)S(1)} %all-to-all-done.1.own), channel_id=1, source_target_pairs={{0,1},{1,0},{2,3},{3,2},{4,5},{5,4},{6,7},{7,6},{8,9},{9,8},{10,11... | collective-permute-start | bytes 2359304 | tf_op jit(solution)/shard_map/ppermute | solution.py:364
  49.6 3.1 %collective-permute-start.7 = (f16[8,16,1152]{2,1,0:T(8,128)(2,1)S(1)}, f16[8,16,1152]{2,1,0:T(8,128)(2,1)S(1)}, u32[]{:S(2)}, u32[]{:S(2)}) collective-permute-start(f16[8,16,1152]{2,1,0:T(8,128)(2,1)S(1)} %slice.9), channel_id=1, source_target_pairs={{0,1},{1,0},{2,3},{3,2},{4,5},{5,4},{6,7},{7,6},{8,9},{9,8},{10,11... | collective-permute-start | bytes 884744 | tf_op jit(solution)/shard_map/ppermute | solution.py:376
  52.8 1.0 copy-start.2
  55.2 3.2 %collective-permute-start.8 = (f16[1,16,2176]{2,1,0:T(8,128)(2,1)S(1)}, f16[1,16,2176]{2,1,0:T(8,128)(2,1)S(1)}, u32[]{:S(2)}, u32[]{:S(2)}) collective-permute-start(f16[1,16,2176]{2,1,0:T(8,128)(2,1)S(1)} %get-tuple-element.51), channel_id=1, source_target_pairs={{0,2},{1,3},{2,0},{3,1},{4,6},{5,7},{6,4},{7,5},{8,10},{9,11},{10,... | collective-permute-start | bytes 208904 | tf_op jit(solution)/shard_map/ppermute | solution.py:404
  58.5 9.2 %collective-permute-start.9 = (f16[2,16,2176]{2,1,0:T(8,128)(2,1)S(1)}, f16[2,16,2176]{2,1,0:T(8,128)(2,1)S(1)}, u32[]{:S(2)}, u32[]{:S(2)}) collective-permute-start(f16[2,16,2176]{2,1,0:T(8,128)(2,1)S(1)} %pad_maximum_fusion.2), channel_id=1, source_target_pairs={{0,4},{1,5},{2,6},{3,7},{4,0},{5,1},{6,2},{7,3},{8,12},{9,13},{10,... | collective-permute-start | bytes 417800 | tf_op jit(solution)/shard_map/ppermute | solution.py:404
  59.4 24.6 %all-to-all-start.2 = ((f16[16,32,512]{2,1,0:T(8,128)(2,1)}), f16[16,32,512]{2,1,0:T(8,128)(2,1)S(1)}, u32[]{:S(2)}, u32[]{:S(2)}) async-start(f16[16,32,512]{2,1,0:T(8,128)(2,1)} %bitcast.7), calls=%async_computation.2 | async-start | bytes 1048576 | tf_op jit(solution)/shard_map/all_to_all | solution.py:398
  67.8 7.7 %collective-permute-start.10 = (f16[4,16,2176]{2,1,0:T(8,128)(2,1)S(1)}, f16[4,16,2176]{2,1,0:T(8,128)(2,1)S(1)}, u32[]{:S(2)}, u32[]{:S(2)}) collective-permute-start(f16[4,16,2176]{2,1,0:T(8,128)(2,1)S(1)} %pad_maximum_fusion.1), channel_id=1, source_target_pairs={{0,12},{1,13},{2,14},{3,15},{4,8},{5,9},{6,10},{7,11},{8,4},{9,5},... | collective-permute-start | bytes 835592 | tf_op jit(solution)/shard_map/ppermute | solution.py:404
  75.6 14.0 %collective-permute-start.11 = (f16[8,16,2176]{2,1,0:T(8,128)(2,1)S(1)}, f16[8,16,2176]{2,1,0:T(8,128)(2,1)}, u32[]{:S(2)}, u32[]{:S(2)}) collective-permute-start(f16[8,16,2176]{2,1,0:T(8,128)(2,1)S(1)} %pad_maximum_fusion), channel_id=1, source_target_pairs={{0,1},{1,0},{2,3},{3,2},{4,5},{5,4},{6,7},{7,6},{8,9},{9,8},{10,11... | collective-permute-start | bytes 1671176 | tf_op jit(solution)/shard_map/ppermute | solution.py:404
  85.8 17.0 %all-to-all-start.3 = ((f16[16,32,384]{2,1,0:T(8,128)(2,1)}), f16[16,32,384]{2,1,0:T(8,128)(2,1)S(1)}, u32[]{:S(2)}, u32[]{:S(2)}) async-start(f16[16,32,384]{2,1,0:T(8,128)(2,1)} %broadcast_in_dim.18), calls=%async_computation.3 | async-start | bytes 786432 | tf_op jit(solution)/shard_map/all_to_all | solution.py:439
  90.8 1.5 %copy-start = (bf16[27,128,256]{2,1,0:T(8,128)(2,1)S(1)}, bf16[27,128,256]{2,1,0:T(8,128)(2,1)}, u32[]{:S(2)}) copy-start(bf16[27,128,256]{2,1,0:T(8,128)(2,1)} %weight.1) | copy-start | bytes 5308420
  103.9 17.0 %all-to-all-start.4 = ((f16[8,448,128]{2,1,0:T(8,128)(2,1)}), f16[8,448,128]{2,1,0:T(8,128)(2,1)S(1)}, u32[]{:S(2)}, u32[]{:S(2)}) async-start(f16[8,448,128]{2,1,0:T(8,128)(2,1)} %broadcast_in_dim.20), calls=%async_computation.4 | async-start | bytes 1835008 | tf_op jit(solution)/shard_map/all_to_all | solution.py:444
  109.4 8.3 %collective-permute-start.12 = (f32[64,128]{1,0:T(8,128)S(1)}, f32[64,128]{1,0:T(8,128)S(1)}, u32[]{:S(2)}, u32[]{:S(2)}) collective-permute-start(f32[64,128]{1,0:T(8,128)S(1)} %get-tuple-element.42), channel_id=1, source_target_pairs={{0,16},{16,32},{32,48},{48,64},{64,80},{80,96},{96,112},{112,128},... | collective-permute-start | bytes 98312 | tf_op jit(solution)/shard_map/ppermute | solution.py:418
  112.3 5.9 %collective-permute-start.13 = (f32[64,128]{1,0:T(8,128)S(1)}, f32[64,128]{1,0:T(8,128)S(1)}, u32[]{:S(2)}, u32[]{:S(2)}) collective-permute-start(f32[64,128]{1,0:T(8,128)S(1)} %get-tuple-element.43), channel_id=1, source_target_pairs={{16,0},{32,16},{48,32},{64,48},{80,64},{96,80},{112,96},{128,112},... | collective-permute-start | bytes 98312 | tf_op jit(solution)/shard_map/ppermute | solution.py:419
  120.9 7.7 %collective-permute-start.14 = (f16[8,448,128]{2,1,0:T(8,128)(2,1)S(1)}, f16[8,448,128]{2,1,0:T(8,128)(2,1)S(1)}, u32[]{:S(2)}, u32[]{:S(2)}) collective-permute-start(f16[8,448,128]{2,1,0:T(8,128)(2,1)S(1)} %all-to-all-done.4), channel_id=1, source_target_pairs={{0,1},{1,0},{2,3},{3,2},{4,5},{5,4},{6,7},{7,6},{8,9},{9,8},{10,11... | collective-permute-start | bytes 2752520 | tf_op jit(solution)/shard_map/ppermute | solution.py:456
  (5 other events, 4.0 us)

commit v2 on v1

v2 whole, which is shorter than its diff:
```python
import functools
import math

import jax
import jax.numpy as jnp
from jax import lax
from jax.experimental import pallas as pl
from jax.experimental.pallas import tpu as pltpu
from jax.sharding import PartitionSpec as P

leak_slope = 0.3
bf16 = jnp.bfloat16
f32 = jnp.float32
f16 = jnp.float16
top = 13.0
planes, rows, cols = 2, 16, 64
lanes = planes * cols
voxels = rows * lanes
block = 16
taps = 27

same_core = [[2 * i + core for i in range(8)] for core in range(2)]
z_swap = [(i, i ^ 2) for i in range(16)]
core_swap = [(i, i ^ 1) for i in range(16)]
share = 88
swaps = ((4,), (12,), (1,))
block_order = [0]
for together in swaps:
    block_order += [other ^ swap for swap in together for other in block_order]
slab_step = [(s * 16 + f, (s + 1) * 16 + f) for s in range(15) for f in range(0, 16, 2)]
slab_step += [((s + 1) * 16 + f, s * 16 + f) for s in range(15) for f in range(1, 16, 2)]


def params():
    return pltpu.CompilerParams(vmem_limit_bytes=48 * 1024 * 1024)


def cost(flops, moved):
    return pl.CostEstimate(flops=flops, bytes_accessed=moved, transcendentals=0)


def shape(dims, dtype):
    return jax.ShapeDtypeStruct(dims, dtype)


def whole(count):
    return [pl.BlockSpec(memory_space=pltpu.VMEM)] * count


def scalar_spec():
    return pl.BlockSpec(memory_space=pltpu.SMEM)


def exponent(value):
    most = jnp.max(jnp.max(jnp.abs(value), axis=0, keepdims=True), axis=1, keepdims=True)
    return jnp.ceil(jnp.log2(jnp.maximum(most, 2.0**-100)))


def weight_kernel(place, weight, ready, own, sent):
    flat = weight[...].astype(f32).reshape(taps * block, 256).T.astype(bf16)
    low, high = flat[:128], flat[128:]
    own[...] = jnp.where(place[0] == 0, low, high)
    sent[...] = jnp.where(place[0] == 0, high, low)


def pack_kernel(place, cot, x, keep, swap):
    core = place[0]
    for plane, out in ((1 - core, keep), (core, swap)):
        field = cot[plane].reshape(rows * block, cols)
        piece = x[plane]
        side = jnp.concatenate(
            [piece[:, :cols], piece[:, cols:], jnp.zeros((2 * cols, cols), bf16)], axis=0
        )
        out[...] = jnp.concatenate([field, side], axis=1)


def message_kernel(pre, x, packed, out):
    value = pre[...].astype(f32).reshape(lanes, 256)
    active = jnp.where(value > 0, value, leak_slope * value).astype(bf16)
    own = x[...].reshape(lanes, 128)
    for i in range(8):
        out[i, 0] = active[:, :128]
        out[i, 1] = active[:, 128:]
        out[i, 2] = own


def shifted_rows(field, b):
    gap = jnp.zeros((field.shape[0], lanes), field.dtype)
    if b == 1:
        return jnp.concatenate([gap, field[:, :-lanes]], axis=1)
    if b == -1:
        return jnp.concatenate([field[:, lanes:], gap], axis=1)
    return field


def shifted_columns(field, c):
    if c == 0:
        return field
    width = field.shape[1]
    col = lax.broadcasted_iota(jnp.int32, field.shape, 1) % cols
    edge = 0 if c == 1 else cols - 1
    return jnp.where(col == edge, jnp.zeros_like(field), pltpu.roll(field, c % width, axis=1))


def fill_columns(own, low, high, out):
    below = low[:, :cols].reshape(rows, block, cols)
    above = high[:, :cols].reshape(rows, block, cols)
    parts = [below, own[0], own[1], above]
    for a in (-1, 0, 1):
        pieces = []
        for r in range(rows):
            pieces += [parts[1 - a][r].astype(f32), parts[2 - a][r].astype(f32)]
        field = jnp.concatenate(
            [jnp.concatenate(pieces[2 * r : 2 * r + 2], axis=1) for r in range(rows)], axis=1
        )
        for c in (-1, 0, 1):
            moved = shifted_columns(field, c).astype(bf16)
            for b in (-1, 0, 1):
                tap = 9 * (a + 1) + 3 * (b + 1) + c + 1
                out[tap * block : (tap + 1) * block, :] = shifted_rows(moved, b)


def back_kernel(place, own, other, here, there, own_w, other_w, out, cot_cols, other_cols):
    core = place[0]
    own_low, own_high = (jnp.where(core == side, here[0], there[1]) for side in range(2))
    other_low, other_high = (jnp.where(core == side, here[1], there[0]) for side in range(2))
    fill_columns(own, own_low, own_high, cot_cols)
    fill_columns(other, other_low, other_high, other_cols)
    total = jnp.dot(own_w[...], cot_cols[...], preferred_element_type=f32)
    total += jnp.dot(other_w[...], other_cols[...], preferred_element_type=f32)
    power = exponent(total)
    out[:, :, :voxels] = (total * jnp.exp2(top - power)).reshape(8, block, voxels)
    rims = [
        jnp.concatenate([pack[0:cols, cols:], pack[cols : 2 * cols, cols:]], axis=1)
        for pack in (own_low, own_high)
    ]
    rim = jnp.concatenate(rims, axis=0).astype(f32)
    rim_power = exponent(rim)
    rim = rim * jnp.exp2(top - rim_power)
    side = [
        jnp.broadcast_to(power, (block, cols)),
        jnp.broadcast_to(rim_power, (block, cols)),
    ] + [rim[g * block : (g + 1) * block] for g in range(8)]
    side = jnp.concatenate(side, axis=1)
    for i in range(8):
        out[i, :, voxels:] = side


def second_kernel(place, cot_cols, own, other, grad, slope, active):
    core = place[0]
    first = place[0] * 128 + place[1] // 2 * block
    for i in range(8):
        for part, side in ((own, core), (other, 1 - core)):
            here = pl.ds(pl.multiple_of((2 * i + side) * lanes, lanes), lanes)
            active[here, 0:128] = part[i, 0]
            active[here, 128:256] = part[i, 1]
    grad[...] = jnp.dot(cot_cols[...], active[...], preferred_element_type=f32)
    positive = jnp.where(active[...].astype(f32) > 0, 1.0, 0.0).astype(bf16)
    mid = lax.broadcasted_iota(jnp.int32, (block, 256), 1)
    row = lax.broadcasted_iota(jnp.int32, (block, 256), 0)
    pick = jnp.where(mid == row + first, 1.0, 0.0).astype(bf16)
    mask = lax.dot_general(pick, positive, (((1,), (1,)), ((), ())), preferred_element_type=f32)
    slope[...] = jnp.where(mask > 0.5, 1.0, leak_slope)


def inputs_kernel(place, own, other, own_rims, other_rims, inputs):
    core = place[0]
    for i in range(8):
        for part, rims, at, side in ((own, own_rims, voxels, core), (other, other_rims, 0, 1 - core)):
            here = pl.ds(pl.multiple_of((2 * i + side) * lanes, lanes), lanes)
            middle = part[i, 2]
            scale = jnp.exp2(rims[i, 0:1, at + cols : at + cols + 1] - top)
            at += 128
            rim = [rims[i, :, at + g * 128 : at + (g + 1) * 128] for g in range(8)]
            rim = (jnp.concatenate(rim, axis=0) * scale).astype(bf16)
            inputs[here, 0:128] = jnp.concatenate([rim[:cols], middle[:cols]], axis=0)
            inputs[here, 128:256] = middle
            inputs[here, 256:384] = jnp.concatenate([middle[cols:], rim[cols:]], axis=0)


def split(value):
    high = value.astype(bf16)
    return high, (value - high.astype(f32)).astype(bf16)


def first_kernel(parts, slope, inputs, second, out, scaled, shifted):
    total = jnp.zeros((block, voxels), f32)
    for i in range(8):
        total = total + parts[i, :, :voxels] * jnp.exp2(parts[i, :, voxels : voxels + 1] - top)
    total = total * slope[...]
    power = exponent(total)
    scaled[:, :voxels] = total * jnp.exp2(top - power)
    scaled[:, voxels:] = jnp.broadcast_to(power, (block, 128))
    for c in (-1, 0, 1):
        pair = split(shifted_columns(total, c))
        for b in (-1, 0, 1):
            at = (3 * (b + 1) + c + 1) * 2 * block
            for k in range(2):
                shifted[at + k * block : at + (k + 1) * block, :] = shifted_rows(pair[k], b)
    grad = jnp.dot(shifted[...], inputs[...], preferred_element_type=f32)
    grad = grad.reshape(9, 2, block, 384)
    grad = grad[:, 0] + grad[:, 1]
    power = exponent(grad.reshape(9 * block, 384))
    grad = grad * jnp.exp2(top - power).reshape(1, 1, 1)
    second_power = exponent(second[...])
    other = second[...] * jnp.exp2(top - second_power)
    pieces = [grad[bc, :, a * 128 : (a + 1) * 128] for a in range(3) for bc in range(9)]
    pieces += [other[:, :128], other[:, 128:], jnp.zeros((share * 16 - 3 * taps * block, 128), f32)]
    flat = jnp.concatenate(pieces, axis=0)
    powers = jnp.concatenate(
        [jnp.broadcast_to(power, (8, cols)), jnp.broadcast_to(second_power, (8, cols))], axis=1
    )
    for i in range(16):
        out[i, :share] = flat[i * share : (i + 1) * share]
        out[i, share:] = powers


def sum_kernel(place, sums, out):
    power = jnp.max(sums[:, share:], axis=0)
    row = lax.broadcasted_iota(jnp.int32, (share, 1), 0) + place[2] * share
    total = jnp.zeros((share, 128), f32)
    for i in range(16):
        change = sums[i, share:] - power - 4.0
        scale = jnp.where(row < taps * block, change[0:1, 0:1], change[0:1, cols : cols + 1])
        total += sums[i, :share] * jnp.exp2(scale)
    out[:share] = total
    out[share:] = power + 4.0


def second_scale_kernel(grad_scale, grad, power, ready, out):
    scale = jnp.exp2(power[0:1, cols : cols + 1] - top) * grad_scale
    out[:, :, :128] = grad[0] * scale.reshape(1, 1, 1)
    out[:, :, 128:] = grad[1] * scale.reshape(1, 1, 1)


def input_kernel(place, blocks, weight, mine, theirs, field):
    filt = place[1]
    for target, out in ((filt, mine), (filt ^ 2, theirs)):
        field[...] = jnp.zeros((256, 3 * lanes), f32)
        for j, other in enumerate(block_order):
            source = filt ^ other
            here = pl.ds(pl.multiple_of((source % 2 * 8 + source // 2) * block, block), block)
            scale = jnp.exp2(blocks[j, 0:1, voxels : voxels + 1] - top)
            for b in range(3):
                row = target + b - 1
                at = pl.multiple_of(jnp.clip(row, 0, rows - 1) * lanes, lanes)
                inside = jnp.logical_and(row >= 0, row < rows)
                piece = jnp.where(inside, blocks[j, :, pl.ds(at, lanes)] * scale, 0.0)
                field[here, b * lanes : (b + 1) * lanes] = piece
        total = jnp.zeros((3 * 128, 2 * lanes), f32)
        for c in (-1, 0, 1):
            pair = split(shifted_columns(field[...], c))
            for b in (-1, 0, 1):
                at = (1 - b) * lanes
                window = jnp.concatenate([half[:, at : at + lanes] for half in pair], axis=1)
                tap = 3 * (b + 1) + c + 1
                taken = jnp.concatenate([weight[9 * a + tap] for a in range(3)], axis=0)
                total += jnp.dot(taken, window, preferred_element_type=f32)
        total = (total[:, :lanes] + total[:, lanes:]).T
        back, middle, ahead = total[:, :128], total[:, 128:256], total[:, 256:]
        out[0:cols] = middle[:cols] + back[cols:]
        out[cols:lanes] = middle[cols:] + ahead[:cols]
        out[lanes : 3 * cols] = back[:cols]
        out[3 * cols :] = ahead[cols:]


def edge_kernel(place, mine, arrived, middle, keep, swap):
    core = place[0]
    middle[...] = mine[0:lanes] + arrived[0:lanes]
    low = mine[lanes : 3 * cols] + arrived[lanes : 3 * cols]
    high = mine[3 * cols :] + arrived[3 * cols :]
    keep[...] = jnp.where(core == 0, high, low)
    swap[...] = jnp.where(core == 0, low, high)


def rim_kernel(place, middle, here, there, out):
    core = place[0]
    low, high = (jnp.where(core == side, here[0], there[...]) for side in range(2))
    out[0:cols] = (middle[0:cols] + low).astype(bf16)
    out[cols:] = (middle[cols:] + high).astype(bf16)


def gather_kernel(grad_scale, place, own, other, out):
    core = place[0]
    start = pl.program_id(0) * 9 * block
    for part, side in ((own, core), (other, 1 - core)):
        power = [
            jnp.broadcast_to(part[i, taps * block : taps * block + 1, 0:1], (block, 1))
            for i in range(8)
        ]
        scale = jnp.exp2(jnp.concatenate(power, axis=0) - top) * grad_scale
        half = pl.ds(pl.multiple_of(side * 128, 128), 128)
        for t in range(9):
            here = pl.ds(pl.multiple_of(start + t * block, block), block)
            out[t, :, half] = (part[:, here].reshape(128, 128) * scale).T


def shards(cotangent, pre_act, layer_input, weight_one, weight_two):
    grad_scale = 1.0 / math.sqrt(voxels * 16)
    filt = lax.axis_index("filt")
    core = filt % 2
    place = jnp.stack([core, filt, lax.axis_index("slab")]).astype(jnp.int32)

    cot = cotangent.transpose(0, 1, 3, 2)
    x = layer_input.reshape(planes, cols, 128)
    pre = pre_act.reshape(planes, cols, 256)
    keep, swap = pl.pallas_call(
        pack_kernel,
        out_shape=[shape((256, 128), bf16)] * 2,
        in_specs=[scalar_spec()] + [pl.BlockSpec()] * 2,
        out_specs=whole(2),
        compiler_params=params(),
        name="pack",
    )(place, cot, x)
    swapped = lax.ppermute(swap, "filt", core_swap)
    here = lax.ppermute(jnp.stack([keep, swapped]), ("slab", "filt"), slab_step)
    there = lax.ppermute(here, "filt", core_swap)
    message = pl.pallas_call(
        message_kernel,
        out_shape=shape((8, 3, 128, 128), bf16),
        in_specs=[pl.BlockSpec()] * 2 + [pl.BlockSpec(memory_space=pl.ANY)],
        out_specs=whole(1)[0],
        compiler_params=params(),
        name="message",
    )(pre, x, swap)
    own_rows = lax.all_to_all(
        message, "filt", split_axis=0, concat_axis=0, tiled=True, axis_index_groups=same_core
    )
    other = lax.ppermute(cot, "filt", core_swap)
    own_w, sent_w = pl.pallas_call(
        weight_kernel,
        out_shape=[shape((128, taps * block), bf16)] * 2,
        in_specs=[scalar_spec()] + [pl.BlockSpec()] + [pl.BlockSpec(memory_space=pl.ANY)],
        out_specs=whole(2),
        compiler_params=params(),
        cost_estimate=cost(12 * 10**9, 1 << 20),
        name="weights",
    )(place, weight_two.transpose(0, 2, 1), here)
    other_w = lax.ppermute(sent_w, "filt", core_swap)

    partial, cot_cols = pl.pallas_call(
        back_kernel,
        out_shape=[shape((8, block, voxels + 1152), f32), shape((taps * block, voxels), bf16)],
        in_specs=[scalar_spec()] + whole(6),
        out_specs=whole(2),
        scratch_shapes=[pltpu.VMEM((taps * block, voxels), bf16)],
        compiler_params=params(),
        cost_estimate=cost(10**10, 4 << 20),
        name="back",
    )(place, cot, other, here, there, own_w, other_w)
    partial = partial.astype(f16)
    own_rows, _ = lax.optimization_barrier((own_rows, partial))
    parts = lax.all_to_all(
        partial, "filt", split_axis=0, concat_axis=0, tiled=True, axis_index_groups=same_core
    )
    other_rows = lax.ppermute(own_rows, "filt", core_swap)
    second, slope = pl.pallas_call(
        second_kernel,
        out_shape=[shape((taps * block, 256), f32), shape((block, voxels), f32)],
        in_specs=[scalar_spec()] + whole(3),
        out_specs=whole(2),
        scratch_shapes=[pltpu.VMEM((voxels, 256), bf16)],
        compiler_params=params(),
        cost_estimate=cost(2 * 432 * 2048 * 256, 6 << 20),
        name="second",
    )(place, cot_cols, own_rows, other_rows)
    parts, _ = lax.optimization_barrier((parts, second))
    rims = parts[:, :, voxels:]
    other_rims = lax.ppermute(rims, "filt", core_swap).astype(f32)
    parts = parts.astype(f32)
    inputs = pl.pallas_call(
        inputs_kernel,
        out_shape=shape((voxels, 384), bf16),
        in_specs=[scalar_spec()] + whole(4),
        out_specs=whole(1)[0],
        compiler_params=params(),
        cost_estimate=cost(10**7, 1 << 20),
        name="inputs",
    )(place, own_rows, other_rows, parts, other_rims)

    merged, scaled = pl.pallas_call(
        first_kernel,
        out_shape=[shape((16, share + 8, 128), f32), shape((block, voxels + 128), f32)],
        in_specs=whole(4),
        out_specs=whole(2),
        scratch_shapes=[pltpu.VMEM((18 * block, voxels), bf16)],
        compiler_params=params(),
        cost_estimate=cost(2 * 288 * 2048 * 384, 6 << 20),
        name="first",
    )(parts, slope, inputs, second)
    merged = merged.astype(f16)
    sums = lax.all_to_all(merged, "slab", split_axis=0, concat_axis=0, tiled=True)

    blocks, _ = lax.optimization_barrier((scaled.astype(f16)[None], inputs))
    for together in swaps:
        arrived = [
            lax.ppermute(blocks, "filt", [(i, i ^ swap) for i in range(16)]) for swap in together
        ]
        blocks = jnp.concatenate([blocks] + arrived, axis=0)
    mine_x0, theirs_x0 = pl.pallas_call(
        input_kernel,
        out_shape=[shape((2 * lanes, 128), f32)] * 2,
        in_specs=[scalar_spec()] + whole(2),
        out_specs=whole(2),
        scratch_shapes=[pltpu.VMEM((256, 3 * lanes), f32)],
        compiler_params=params(),
        cost_estimate=cost(4 * 128 * 256 * 256 * taps, 4 << 20),
        name="input",
    )(place, blocks.astype(f32), weight_one)
    arrived_x0 = lax.ppermute(theirs_x0, "filt", z_swap)
    mine = pl.pallas_call(
        sum_kernel,
        out_shape=shape((share + 8, 128), f32),
        in_specs=[scalar_spec()] + whole(1),
        out_specs=whole(1)[0],
        compiler_params=params(),
        name="sum",
    )(place, sums.astype(f32))
    near = jnp.broadcast_to(mine.astype(f16)[None], (16, share + 8, 128))
    near = lax.all_to_all(near, "slab", split_axis=0, concat_axis=0, tiled=True)
    near, arrived_x0 = lax.optimization_barrier((near, arrived_x0))
    middle, keep, swap = pl.pallas_call(
        edge_kernel,
        out_shape=[shape((lanes, 128), f32)] + [shape((cols, 128), f32)] * 2,
        in_specs=[scalar_spec()] + whole(2),
        out_specs=whole(3),
        compiler_params=params(),
        name="edge",
    )(place, mine_x0, arrived_x0)
    swapped = lax.ppermute(swap, "filt", core_swap)
    rims = lax.ppermute(jnp.stack([keep, swapped]), ("slab", "filt"), slab_step)
    other_rim = lax.ppermute(rims[1], "filt", core_swap)
    grad_x0 = pl.pallas_call(
        rim_kernel,
        out_shape=shape((lanes, 128), bf16),
        in_specs=[scalar_spec()] + whole(3),
        out_specs=whole(1)[0],
        compiler_params=params(),
        name="rim",
    )(place, middle, rims, other_rim).reshape(planes, 1, cols, 128)
    flat = near[:, :share].reshape(16 * share, 128)
    power = near[0, share:]
    wide = jnp.concatenate([flat[: taps * block], power], axis=0)
    wide = jnp.broadcast_to(wide[None], (8, taps * block + 8, 128))
    wide = lax.all_to_all(
        wide, "filt", split_axis=0, concat_axis=0, tiled=True, axis_index_groups=same_core
    )
    wide, grad_x0 = lax.optimization_barrier((wide, grad_x0))
    other_wide = lax.ppermute(wide, "filt", core_swap)
    own_wide = wide.astype(f32)
    grad_w2 = pl.pallas_call(
        functools.partial(second_scale_kernel, grad_scale),
        out_shape=shape((taps, block, 256), f32),
        in_specs=whole(2) + [pl.BlockSpec(memory_space=pl.ANY)],
        out_specs=whole(1)[0],
        compiler_params=params(),
        cost_estimate=cost(5 * 10**9, 1 << 20),
        name="second_scale",
    )(
        flat[taps * block : 3 * taps * block].reshape(2, taps, block, 128).astype(f32),
        power.astype(f32),
        own_wide,
    ).transpose(0, 2, 1)
    grad_w1 = pl.pallas_call(
        functools.partial(gather_kernel, grad_scale),
        out_shape=shape((taps, 128, 256), f32),
        grid=(3,),
        in_specs=[scalar_spec()] + whole(2),
        out_specs=pl.BlockSpec((9, 128, 256), lambda i: (i, 0, 0)),
        compiler_params=params(),
        name="gather",
    )(place, own_wide, other_wide.astype(f32))
    return (grad_w2, grad_w1, grad_x0)


def solution(mesh):
    return jax.shard_map(
        shards,
        mesh=mesh,
        in_specs=(
            P("slab", None, None, "filt"),
            P("slab", "filt", None, None),
            P("slab", "filt", None, None),
            P(),
            P(None, None, "filt"),
        ),
        out_specs=(P(None, None, "filt"), P(), P("slab", "filt", None, None)),
        check_vma=False,
    )
```

time: 133 us -> 126 us (0.947)
  waiting for transfers between devices: 40.8 us -> 37.2 us
  local copies, waits for them, and re-layouts: 9.66 us -> 7.31 us
    all_to_all x1, waiting for transfers between devices: 9.04 us -> 2.68 us  [shards(): near = lax.all_to_all(near, 'slab', split_axis=0, concat_axis=0, tiled=True)]
    ppermute x11, waiting for transfers between devices: 15.5 us -> 21.6 us  [the longest x1 8.23 us: shards(): arrived_x0 = lax.ppermute(theirs_x0, 'filt', z_swap)]
    all_to_all x1, waiting for transfers between devices: 7.58 us -> 2.05 us  [shards(): lax.all_to_all(partial, 'filt', split_axis=0, concat_axis=0, tiled=True,...]
    all_to_all x1, starting transfers between devices: 8.22 us -> 12.9 us  [shards(): lax.all_to_all(merged, 'slab', split_axis=0, concat_axis=0, tiled=True)]
    all_to_all x1, starting transfers between devices: 9.91 us -> 5.33 us  [shards(): lax.all_to_all(partial, 'filt', split_axis=0, concat_axis=0, tiled=True,...]
    ppermute x11, starting transfers between devices: 18.9 us -> 22.5 us  [the longest x2 7.57 us: shards(): swapped = lax.ppermute(swap, 'filt', core_swap)]
    ppermute x1, starting transfers between devices: 4.52 us -> 1.59 us  [shards(): other_wide = lax.ppermute(wide, 'filt', core_swap)]
    ppermute x1, starting transfers between devices: 0.63 us -> 3.51 us  [shards(): other_rows = lax.ppermute(own_rows, 'filt', core_swap)]
  transfers between devices with their start and end apart: 20 -> 20, of which waited for: 12 -> 13; matrix products, arithmetic and copies ran while one was open for 5% -> 3% of each run, Pallas kernels for 8% -> 9%
where the time goes in v2:
time: 126 us; the launch traced here: 125 us
  starting transfers between devices  58 us (46%)
  waiting for transfers between devices  37.2 us (30%)
  Pallas kernels  17.8 us (14%)
  local copies, waits for them, and re-layouts  7.31 us (6%)
  other arithmetic  3.79 us (3%)
    all_to_all x1, starting transfers between devices, shards(): lax.all_to_all(merged, 'slab', split_axis=0, concat_axis=0, tiled=True)  12.9 us
    ppermute x1, waiting for transfers between devices, shards(): arrived_x0 = lax.ppermute(theirs_x0, 'filt', z_swap)  8.23 us
    ppermute x2, starting transfers between devices, shards(): swapped = lax.ppermute(swap, 'filt', core_swap)  7.57 us
    all_to_all x1, waiting for transfers between devices, shards(): lax.all_to_all(merged, 'slab', split_axis=0, concat_axis=0, tiled=True)  6.9 us
    all_to_all x1, starting transfers between devices, shards(): lax.all_to_all(partial, 'filt', split_axis=0, concat_axis=0, tiled=True,...  5.33 us
    ppermute x3, waiting for transfers between devices, shards(): lax.ppermute(blocks, 'filt', [(i, i ^ swap) for i in range(16)])  5.03 us
    ppermute x1, waiting for transfers between devices, shards(): rims = lax.ppermute(jnp.stack([keep, swapped]), ('slab', 'filt'), slab_step)  4.9 us
    ppermute x1, starting transfers between devices, shards(): other_rims = lax.ppermute(rims, 'filt', core_swap).astype(f32)  4.63 us
  transfers between devices with their start and end apart: 20, of which 13 were waited for; matrix products, arithmetic and copies ran while one was open for 3% of the time, Pallas kernels for 9%

profile of v2, /device:TPU:1, one launch (start us, length us, event | category | flops | bytes accessed | tf_op | source)
XLA Modules:
  0.0 125.0 jit_solution(2970225048961383875)
XLA Ops:
  3.1 3.3 %collective-permute-start.1 = (bf16[256,128]{1,0:T(8,128)(2,1)S(1)}, bf16[256,128]{1,0:T(8,128)(2,1)S(1)}, u32[]{:S(2)}, u32[]{:S(2)}) collective-permute-start(bf16[256,128]{1,0:T(8,128)(2,1)S(1)} %get-tuple-element.26.packed), channel_id=1, source_target_pairs={{0,1},{1,0},{2,3},{3,2},{4,5},{5,4},{6,7},{7,6},{8,9},{9,8},{10,11... | collective-permute-start | bytes 196616 | tf_op jit(solution)/shard_map/ppermute | solution.py:315
  11.2 3.6 %all-to-all-start.1 = ((bf16[8,3,128,128]{3,2,1,0:T(8,128)(2,1)}), bf16[8,3,128,128]{3,2,1,0:T(8,128)(2,1)S(1)}, u32[]{:S(2)}, u32[]{:S(2)}) async-start(bf16[8,3,128,128]{3,2,1,0:T(8,128)(2,1)} %message.1), calls=%async_computation.1 | async-start | bytes 1572864 | tf_op jit(solution)/shard_map/all_to_all | solution.py:326
  15.3 4.1 %collective-permute-start.3 = (bf16[2,256,128]{2,1,0:T(8,128)(2,1)S(1)}, bf16[2,256,128]{2,1,0:T(8,128)(2,1)S(1)}, u32[]{:S(2)}, u32[]{:S(2)}) collective-permute-start(bf16[2,256,128]{2,1,0:T(8,128)(2,1)S(1)} %collective-permute-done.2.ready.here), channel_id=1, source_target_pairs={{0,1},{1,0},{2,3},{3,2},{4,5},{5,4},{6,7},{7,6},{8,9},{9,8},{10,11... | collective-permute-start | bytes 393224 | tf_op jit(solution)/shard_map/ppermute | solution.py:317
  21.8 2.2 %back.1 = (f32[8,16,3200]{2,1,0:T(8,128)S(1)}, bf16[432,2048]{1,0:T(8,128)(2,1)S(1)}) custom-call(s32[3]{0:T(128)S(1)} %pad_add_fusion.place, bf16[2,16,16,64]{3,2,1,0:T(8,128)(2,1)S(1)} %bitcast.27, bf16[2,16,16,64]{3,2,1,0:T(8,128)(2,1)S(1)} %collective-permute-done.other, bf16[2,256,128]{2,1,0:T(8,128)(2,1)S(1)} %collective-permute-done.2.ready.here, ...), custom_call_target="tpu_custom_call" | custom-call | flops 10000000000 | bytes 4194304 | tf_op jit(solution)/shard_map/back/pallas_call | solution.py:341
  24.9 5.3 %all-to-all-start = ((f16[8,16,3200]{2,1,0:T(8,128)(2,1)}), f16[8,16,3200]{2,1,0:T(8,128)(2,1)}, u32[]{:S(2)}, u32[]{:S(2)}) async-start(f16[8,16,3200]{2,1,0:T(8,128)(2,1)} %convert_element_type.38), calls=%async_computation | async-start | bytes 1638400 | tf_op jit(solution)/shard_map/all_to_all | solution.py:353
  30.3 3.5 %collective-permute-start.5 = (bf16[8,3,128,128]{3,2,1,0:T(8,128)(2,1)S(1)}, bf16[8,3,128,128]{3,2,1,0:T(8,128)(2,1)S(1)}, u32[]{:S(2)}, u32[]{:S(2)}) collective-permute-start(bf16[8,3,128,128]{3,2,1,0:T(8,128)(2,1)S(1)} %all-to-all-done.1.own), channel_id=1, source_target_pairs={{0,1},{1,0},{2,3},{3,2},{4,5},{5,4},{6,7},{7,6},{8,9},{9,8},{10,11... | collective-permute-start | bytes 2359304 | tf_op jit(solution)/shard_map/ppermute | solution.py:356
  33.8 1.9 %collective-permute-done.5.other = bf16[8,3,128,128]{3,2,1,0:T(8,128)(2,1)S(1)} collective-permute-done((bf16[8,3,128,128]{3,2,1,0:T(8,128)(2,1)S(1)}, bf16[8,3,128,128]{3,2,1,0:T(8,128)(2,1)S(1)}, u32[]{:S(2)}, u32[]{:S(2)}) %collective-permute-start.5) | collective-permute-done | bytes 786464 | tf_op jit(solution)/shard_map/ppermute | solution.py:356
  35.7 1.6 %second.1 = (f32[432,256]{1,0:T(8,128)S(1)}, f32[16,2048]{1,0:T(8,128)S(1)}) custom-call(s32[3]{0:T(128)S(1)} %pad_add_fusion.place, bf16[432,2048]{1,0:T(8,128)(2,1)S(1)} %get-tuple-element.30.cot_cols, bf16[8,3,128,128]{3,2,1,0:T(8,128)(2,1)S(1)} %all-to-all-done.1.own, bf16[8,3,128,128]{3,2,1,0:T(8,128)(2,1)S(1)} %collective-permute-done.5.other), custom_call_target="tpu_custom_call" | custom-call | flops 452984832 | bytes 6291456 | tf_op jit(solution)/shard_map/second/pallas_call | solution.py:357
  38.1 2.0 %all-to-all-done = f16[8,16,3200]{2,1,0:T(8,128)(2,1)} async-done(((f16[8,16,3200]{2,1,0:T(8,128)(2,1)}), f16[8,16,3200]{2,1,0:T(8,128)(2,1)}, u32[]{:S(2)}, u32[]{:S(2)}) %all-to-all-start) | async-done | bytes 819232 | tf_op jit(solution)/shard_map/all_to_all | solution.py:353
  41.1 4.6 %collective-permute-start.6 = (f16[8,16,1152]{2,1,0:T(8,128)(2,1)S(1)}, f16[8,16,1152]{2,1,0:T(8,128)(2,1)S(1)}, u32[]{:S(2)}, u32[]{:S(2)}) collective-permute-start(f16[8,16,1152]{2,1,0:T(8,128)(2,1)S(1)} %slice.18), channel_id=1, source_target_pairs={{0,1},{1,0},{2,3},{3,2},{4,5},{5,4},{6,7},{7,6},{8,9},{9,8},{10,11... | collective-permute-start | bytes 884744 | tf_op jit(solution)/shard_map/ppermute | solution.py:369
  50.3 12.9 %all-to-all-start.2 = ((f16[16,96,128]{2,1,0:T(8,128)(2,1)}), f16[16,96,128]{2,1,0:T(8,128)(2,1)S(1)}, u32[]{:S(2)}, u32[]{:S(2)}) async-start(f16[16,96,128]{2,1,0:T(8,128)(2,1)} %convert_element_type.41), calls=%async_computation.2 | async-start | bytes 786432 | tf_op jit(solution)/shard_map/all_to_all | solution.py:392
  64.2 5.0 %collective-permute-done.8 = f16[2,16,2176]{2,1,0:T(8,128)(2,1)S(1)} collective-permute-done((f16[2,16,2176]{2,1,0:T(8,128)(2,1)S(1)}, f16[2,16,2176]{2,1,0:T(8,128)(2,1)S(1)}, u32[]{:S(2)}, u32[]{:S(2)}) %collective-permute-start.8) | collective-permute-done | bytes 139296 | tf_op jit(solution)/shard_map/ppermute | solution.py:397
  69.3 1.5 %collective-permute-start.9 = (f16[4,16,2176]{2,1,0:T(8,128)(2,1)S(1)}, f16[4,16,2176]{2,1,0:T(8,128)(2,1)S(1)}, u32[]{:S(2)}, u32[]{:S(2)}) collective-permute-start(f16[4,16,2176]{2,1,0:T(8,128)(2,1)S(1)} %pad_maximum_fusion), channel_id=1, source_target_pairs={{0,1},{1,0},{2,3},{3,2},{4,5},{5,4},{6,7},{7,6},{8,9},{9,8},{10,11... | collective-permute-start | bytes 835592 | tf_op jit(solution)/shard_map/ppermute | solution.py:397
  70.8 6.9 %all-to-all-done.2 = f16[16,96,128]{2,1,0:T(8,128)(2,1)S(1)} async-done(((f16[16,96,128]{2,1,0:T(8,128)(2,1)}), f16[16,96,128]{2,1,0:T(8,128)(2,1)S(1)}, u32[]{:S(2)}, u32[]{:S(2)}) %all-to-all-start.2) | async-done | bytes 393248 | tf_op jit(solution)/shard_map/all_to_all | solution.py:392
  77.8 1.4 %sum.1 = f32[96,128]{1,0:T(8,128)S(1)} custom-call(s32[3]{0:T(128)S(1)} %pad_add_fusion.place, f32[16,96,128]{2,1,0:T(8,128)S(1)} %convert_element_type.42.sums), custom_call_target="tpu_custom_call" | custom-call | tf_op jit(solution)/shard_map/sum/pallas_call | solution.py:411
  80.0 4.2 %all-to-all-start.3 = ((f16[16,96,128]{2,1,0:T(8,128)(2,1)}), f16[16,96,128]{2,1,0:T(8,128)(2,1)S(1)}, u32[]{:S(2)}, u32[]{:S(2)}) async-start(f16[16,96,128]{2,1,0:T(8,128)(2,1)} %broadcast_in_dim.6), calls=%async_computation.3 | async-start | bytes 786432 | tf_op jit(solution)/shard_map/all_to_all | solution.py:420
  84.3 2.1 %input.1 = (f32[256,128]{1,0:T(8,128)S(1)}, f32[256,128]{1,0:T(8,128)S(1)}) custom-call(s32[3]{0:T(128)S(1)} %pad_add_fusion.place, f32[8,16,2176]{2,1,0:T(8,128)S(1)} %maximum_convert_fusion.blocks, bf16[27,128,256]{2,1,0:T(8,128)(2,1)S(1)} %copy-done.7), custom_call_target="tpu_custom_call" | custom-call | flops 905969664 | bytes 4194304 | tf_op jit(solution)/shard_map/input/pallas_call | solution.py:400
  87.5 8.2 %collective-permute-done.10.arrived = f32[256,128]{1,0:T(8,128)S(1)} collective-permute-done((f32[256,128]{1,0:T(8,128)S(1)}, f32[256,128]{1,0:T(8,128)S(1)}, u32[]{:S(2)}, u32[]{:S(2)}) %collective-permute-start.10) | collective-permute-done | bytes 131104 | tf_op jit(solution)/shard_map/ppermute | solution.py:410
  95.7 2.7 %all-to-all-done.3 = f16[16,96,128]{2,1,0:T(8,128)(2,1)S(1)} async-done(((f16[16,96,128]{2,1,0:T(8,128)(2,1)}), f16[16,96,128]{2,1,0:T(8,128)(2,1)S(1)}, u32[]{:S(2)}, u32[]{:S(2)}) %all-to-all-start.3) | async-done | bytes 393248 | tf_op jit(solution)/shard_map/all_to_all | solution.py:420
  99.6 3.8 %all-to-all-start.4 = ((f16[8,440,128]{2,1,0:T(8,128)(2,1)}), f16[8,440,128]{2,1,0:T(8,128)(2,1)S(1)}, u32[]{:S(2)}, u32[]{:S(2)}) async-start(f16[8,440,128]{2,1,0:T(8,128)(2,1)} %broadcast_in_dim.8), calls=%async_computation.4 | async-start | bytes 1802240 | tf_op jit(solution)/shard_map/all_to_all | solution.py:445
  104.0 4.3 %collective-permute-start.11 = (f32[64,128]{1,0:T(8,128)S(1)}, f32[64,128]{1,0:T(8,128)S(1)}, u32[]{:S(2)}, u32[]{:S(2)}) collective-permute-start(f32[64,128]{1,0:T(8,128)S(1)} %get-tuple-element.44), channel_id=1, source_target_pairs={{0,1},{1,0},{2,3},{3,2},{4,5},{5,4},{6,7},{7,6},{8,9},{9,8},{10,11... | collective-permute-start | bytes 98312 | tf_op jit(solution)/shard_map/ppermute | solution.py:430
  110.4 4.9 %collective-permute-done.12.here = f32[2,64,128]{2,1,0:T(8,128)S(1)} collective-permute-done((f32[2,64,128]{2,1,0:T(8,128)S(1)}, f32[2,64,128]{2,1,0:T(8,128)S(1)}, u32[]{:S(2)}, u32[]{:S(2)}) %collective-permute-start.12) | collective-permute-done | bytes 65568 | tf_op jit(solution)/shard_map/ppermute | solution.py:431
  117.7 1.6 %collective-permute-start.14 = (f16[8,440,128]{2,1,0:T(8,128)(2,1)S(1)}, f16[8,440,128]{2,1,0:T(8,128)(2,1)S(1)}, u32[]{:S(2)}, u32[]{:S(2)}) collective-permute-start(f16[8,440,128]{2,1,0:T(8,128)(2,1)S(1)} %all-to-all-done.4), channel_id=1, source_target_pairs={{0,1},{1,0},{2,3},{3,2},{4,5},{5,4},{6,7},{7,6},{8,9},{9,8},{10,11... | collective-permute-start | bytes 2703368 | tf_op jit(solution)/shard_map/ppermute | solution.py:449
  121.5 3.5 %gather.1 = f32[27,128,256]{2,1,0:T(8,128)} custom-call(s32[3]{0:T(128)S(1)} %pad_add_fusion.place, f32[8,440,128]{2,1,0:T(8,128)S(1)} %convert_element_type.49.ready.own, f32[8,440,128]{2,1,0:T(8,128)S(1)} %convert_element_type.50.other), custom_call_target="tpu_custom_call" | custom-call | tf_op jit(solution)/shard_map/gather/pallas_call | solution.py:464
  (72 shorter events, 28.8 us)
Async XLA Ops:
  0.7 0.9 copy-start.2
  2.4 17.1 %copy-start.8 = (bf16[27,256,16]{1,2,0:T(8,128)(2,1)S(1)}, bf16[27,256,16]{1,2,0:T(8,128)(2,1)}, u32[]{:S(2)}) copy-start(bf16[27,256,16]{1,2,0:T(8,128)(2,1)} %param.9) | copy-start | bytes 663556
  3.1 4.2 %collective-permute-start.1 = (bf16[256,128]{1,0:T(8,128)(2,1)S(1)}, bf16[256,128]{1,0:T(8,128)(2,1)S(1)}, u32[]{:S(2)}, u32[]{:S(2)}) collective-permute-start(bf16[256,128]{1,0:T(8,128)(2,1)S(1)} %get-tuple-element.26.packed), channel_id=1, source_target_pairs={{0,1},{1,0},{2,3},{3,2},{4,5},{5,4},{6,7},{7,6},{8,9},{9,8},{10,11... | collective-permute-start | bytes 196616 | tf_op jit(solution)/shard_map/ppermute | solution.py:315
  7.3 8.0 %collective-permute-start.2 = (bf16[2,256,128]{2,1,0:T(8,128)(2,1)S(1)}, bf16[2,256,128]{2,1,0:T(8,128)(2,1)S(1)}, u32[]{:S(2)}, u32[]{:S(2)}) collective-permute-start(bf16[2,256,128]{2,1,0:T(8,128)(2,1)S(1)} %pad_maximum_fusion.2), channel_id=1, source_target_pairs={{0,16},{2,18},{4,20},{6,22},{8,24},{10,26},{12,28},{14,30},{16,32}... | collective-permute-start | bytes 393224 | tf_op jit(solution)/shard_map/ppermute | solution.py:316
  11.2 13.8 %all-to-all-start.1 = ((bf16[8,3,128,128]{3,2,1,0:T(8,128)(2,1)}), bf16[8,3,128,128]{3,2,1,0:T(8,128)(2,1)S(1)}, u32[]{:S(2)}, u32[]{:S(2)}) async-start(bf16[8,3,128,128]{3,2,1,0:T(8,128)(2,1)} %message.1), calls=%async_computation.1 | async-start | bytes 1572864 | tf_op jit(solution)/shard_map/all_to_all | solution.py:326
  15.3 6.4 %collective-permute-start.3 = (bf16[2,256,128]{2,1,0:T(8,128)(2,1)S(1)}, bf16[2,256,128]{2,1,0:T(8,128)(2,1)S(1)}, u32[]{:S(2)}, u32[]{:S(2)}) collective-permute-start(bf16[2,256,128]{2,1,0:T(8,128)(2,1)S(1)} %collective-permute-done.2.ready.here), channel_id=1, source_target_pairs={{0,1},{1,0},{2,3},{3,2},{4,5},{5,4},{6,7},{7,6},{8,9},{9,8},{10,11... | collective-permute-start | bytes 393224 | tf_op jit(solution)/shard_map/ppermute | solution.py:317
  20.1 1.6 %collective-permute-start.4 = (bf16[128,432]{1,0:T(8,128)(2,1)S(1)}, bf16[128,432]{1,0:T(8,128)(2,1)S(1)}, u32[]{:S(2)}, u32[]{:S(2)}) collective-permute-start(bf16[128,432]{1,0:T(8,128)(2,1)S(1)} %get-tuple-element.28), channel_id=1, source_target_pairs={{0,1},{1,0},{2,3},{3,2},{4,5},{5,4},{6,7},{7,6},{8,9},{9,8},{10,11... | collective-permute-start | bytes 331784 | tf_op jit(solution)/shard_map/ppermute | solution.py:339
  20.3 1.4 %collective-permute-start = (bf16[2,16,16,64]{3,2,1,0:T(8,128)(2,1)S(1)}, bf16[2,16,16,64]{3,2,1,0:T(8,128)(2,1)S(1)}, u32[]{:S(2)}, u32[]{:S(2)}) collective-permute-start(bf16[2,16,16,64]{3,2,1,0:T(8,128)(2,1)S(1)} %bitcast.26), channel_id=1, source_target_pairs={{0,1},{1,0},{2,3},{3,2},{4,5},{5,4},{6,7},{7,6},{8,9},{9,8},{10,11... | collective-permute-start | bytes 196616 | tf_op jit(solution)/shard_map/ppermute | solution.py:329
  24.9 15.2 %all-to-all-start = ((f16[8,16,3200]{2,1,0:T(8,128)(2,1)}), f16[8,16,3200]{2,1,0:T(8,128)(2,1)}, u32[]{:S(2)}, u32[]{:S(2)}) async-start(f16[8,16,3200]{2,1,0:T(8,128)(2,1)} %convert_element_type.38), calls=%async_computation | async-start | bytes 1638400 | tf_op jit(solution)/shard_map/all_to_all | solution.py:353
  30.3 5.4 %collective-permute-start.5 = (bf16[8,3,128,128]{3,2,1,0:T(8,128)(2,1)S(1)}, bf16[8,3,128,128]{3,2,1,0:T(8,128)(2,1)S(1)}, u32[]{:S(2)}, u32[]{:S(2)}) collective-permute-start(bf16[8,3,128,128]{3,2,1,0:T(8,128)(2,1)S(1)} %all-to-all-done.1.own), channel_id=1, source_target_pairs={{0,1},{1,0},{2,3},{3,2},{4,5},{5,4},{6,7},{7,6},{8,9},{9,8},{10,11... | collective-permute-start | bytes 2359304 | tf_op jit(solution)/shard_map/ppermute | solution.py:356
  41.1 5.9 %collective-permute-start.6 = (f16[8,16,1152]{2,1,0:T(8,128)(2,1)S(1)}, f16[8,16,1152]{2,1,0:T(8,128)(2,1)S(1)}, u32[]{:S(2)}, u32[]{:S(2)}) collective-permute-start(f16[8,16,1152]{2,1,0:T(8,128)(2,1)S(1)} %slice.18), channel_id=1, source_target_pairs={{0,1},{1,0},{2,3},{3,2},{4,5},{5,4},{6,7},{7,6},{8,9},{9,8},{10,11... | collective-permute-start | bytes 884744 | tf_op jit(solution)/shard_map/ppermute | solution.py:369
  47.1 1.0 copy-start.1
  49.4 13.8 %collective-permute-start.7 = (f16[1,16,2176]{2,1,0:T(8,128)(2,1)S(1)}, f16[1,16,2176]{2,1,0:T(8,128)(2,1)S(1)}, u32[]{:S(2)}, u32[]{:S(2)}) collective-permute-start(f16[1,16,2176]{2,1,0:T(8,128)(2,1)S(1)} %convert_bitcast_fusion), channel_id=1, source_target_pairs={{0,4},{1,5},{2,6},{3,7},{4,0},{5,1},{6,2},{7,3},{8,12},{9,13},{10,... | collective-permute-start | bytes 208904 | tf_op jit(solution)/shard_map/ppermute | solution.py:397
  50.3 27.4 %all-to-all-start.2 = ((f16[16,96,128]{2,1,0:T(8,128)(2,1)}), f16[16,96,128]{2,1,0:T(8,128)(2,1)S(1)}, u32[]{:S(2)}, u32[]{:S(2)}) async-start(f16[16,96,128]{2,1,0:T(8,128)(2,1)} %convert_element_type.41), calls=%async_computation.2 | async-start | bytes 786432 | tf_op jit(solution)/shard_map/all_to_all | solution.py:392
  63.3 5.9 %collective-permute-start.8 = (f16[2,16,2176]{2,1,0:T(8,128)(2,1)S(1)}, f16[2,16,2176]{2,1,0:T(8,128)(2,1)S(1)}, u32[]{:S(2)}, u32[]{:S(2)}) collective-permute-start(f16[2,16,2176]{2,1,0:T(8,128)(2,1)S(1)} %pad_maximum_fusion.1), channel_id=1, source_target_pairs={{0,12},{1,13},{2,14},{3,15},{4,8},{5,9},{6,10},{7,11},{8,4},{9,5},... | collective-permute-start | bytes 417800 | tf_op jit(solution)/shard_map/ppermute | solution.py:397
  69.3 14.9 %collective-permute-start.9 = (f16[4,16,2176]{2,1,0:T(8,128)(2,1)S(1)}, f16[4,16,2176]{2,1,0:T(8,128)(2,1)S(1)}, u32[]{:S(2)}, u32[]{:S(2)}) collective-permute-start(f16[4,16,2176]{2,1,0:T(8,128)(2,1)S(1)} %pad_maximum_fusion), channel_id=1, source_target_pairs={{0,1},{1,0},{2,3},{3,2},{4,5},{5,4},{6,7},{7,6},{8,9},{9,8},{10,11... | collective-permute-start | bytes 835592 | tf_op jit(solution)/shard_map/ppermute | solution.py:397
  77.8 6.5 %copy-start.7 = (bf16[27,128,256]{2,1,0:T(8,128)(2,1)S(1)}, bf16[27,128,256]{2,1,0:T(8,128)(2,1)}, u32[]{:S(2)}) copy-start(bf16[27,128,256]{2,1,0:T(8,128)(2,1)} %weight.1) | copy-start | bytes 5308420
  80.0 18.4 %all-to-all-start.3 = ((f16[16,96,128]{2,1,0:T(8,128)(2,1)}), f16[16,96,128]{2,1,0:T(8,128)(2,1)S(1)}, u32[]{:S(2)}, u32[]{:S(2)}) async-start(f16[16,96,128]{2,1,0:T(8,128)(2,1)} %broadcast_in_dim.6), calls=%async_computation.3 | async-start | bytes 786432 | tf_op jit(solution)/shard_map/all_to_all | solution.py:420
  86.4 9.3 %collective-permute-start.10 = (f32[256,128]{1,0:T(8,128)S(1)}, f32[256,128]{1,0:T(8,128)S(1)}, u32[]{:S(2)}, u32[]{:S(2)}) collective-permute-start(f32[256,128]{1,0:T(8,128)S(1)} %get-tuple-element.38), channel_id=1, source_target_pairs={{0,2},{1,3},{2,0},{3,1},{4,6},{5,7},{6,4},{7,5},{8,10},{9,11},{10,... | collective-permute-start | bytes 393224 | tf_op jit(solution)/shard_map/ppermute | solution.py:410
  99.6 18.1 %all-to-all-start.4 = ((f16[8,440,128]{2,1,0:T(8,128)(2,1)}), f16[8,440,128]{2,1,0:T(8,128)(2,1)S(1)}, u32[]{:S(2)}, u32[]{:S(2)}) async-start(f16[8,440,128]{2,1,0:T(8,128)(2,1)} %broadcast_in_dim.8), calls=%async_computation.4 | async-start | bytes 1802240 | tf_op jit(solution)/shard_map/all_to_all | solution.py:445
  104.0 5.1 %collective-permute-start.11 = (f32[64,128]{1,0:T(8,128)S(1)}, f32[64,128]{1,0:T(8,128)S(1)}, u32[]{:S(2)}, u32[]{:S(2)}) collective-permute-start(f32[64,128]{1,0:T(8,128)S(1)} %get-tuple-element.44), channel_id=1, source_target_pairs={{0,1},{1,0},{2,3},{3,2},{4,5},{5,4},{6,7},{7,6},{8,9},{9,8},{10,11... | collective-permute-start | bytes 98312 | tf_op jit(solution)/shard_map/ppermute | solution.py:430
  109.2 6.2 %collective-permute-start.12 = (f32[2,64,128]{2,1,0:T(8,128)S(1)}, f32[2,64,128]{2,1,0:T(8,128)S(1)}, u32[]{:S(2)}, u32[]{:S(2)}) collective-permute-start(f32[2,64,128]{2,1,0:T(8,128)S(1)} %pad_maximum_fusion.4), channel_id=1, source_target_pairs={{0,16},{2,18},{4,20},{6,22},{8,24},{10,26},{12,28},{14,30},{16,32}... | collective-permute-start | bytes 196616 | tf_op jit(solution)/shard_map/ppermute | solution.py:431
  115.4 1.2 collective-permute-start.13
  117.7 3.7 %collective-permute-start.14 = (f16[8,440,128]{2,1,0:T(8,128)(2,1)S(1)}, f16[8,440,128]{2,1,0:T(8,128)(2,1)S(1)}, u32[]{:S(2)}, u32[]{:S(2)}) collective-permute-start(f16[8,440,128]{2,1,0:T(8,128)(2,1)S(1)} %all-to-all-done.4), channel_id=1, source_target_pairs={{0,1},{1,0},{2,3},{3,2},{4,5},{5,4},{6,7},{7,6},{8,9},{9,8},{10,11... | collective-permute-start | bytes 2703368 | tf_op jit(solution)/shard_map/ppermute | solution.py:449
  (5 other events, 4.0 us)

commit v3 on v2

--- a/solution.py
+++ b/solution.py
@@ -216,14 +216,20 @@
 
 
 def sum_kernel(place, sums, out):
-    power = jnp.max(sums[:, share:], axis=0)
-    row = lax.broadcasted_iota(jnp.int32, (share, 1), 0) + place[2] * share
-    total = jnp.zeros((share, 128), f32)
+    power = sums[0, share:]
+    for i in range(1, 16):
+        power = jnp.maximum(power, sums[i, share:])
+    left = lax.broadcasted_iota(jnp.int32, (8, 128), 1) < cols
+    totals = [jnp.zeros((8, 128), f32)] * (share // 8)
     for i in range(16):
-        change = sums[i, share:] - power - 4.0
-        scale = jnp.where(row < taps * block, change[0:1, 0:1], change[0:1, cols : cols + 1])
-        total += sums[i, :share] * jnp.exp2(scale)
-    out[:share] = total
+        scale = jnp.exp2(sums[i, share:] - power - 4.0)
+        turned = pltpu.roll(scale, cols, axis=1)
+        first, second = jnp.where(left, scale, turned), jnp.where(left, turned, scale)
+        for k in range(share // 8):
+            here = jnp.where(place[2] * share + 8 * k < taps * block, first, second)
+            totals[k] += sums[i, 8 * k : 8 * k + 8] * here
+    for k in range(share // 8):
+        out[8 * k : 8 * k + 8] = totals[k]
     out[share:] = power + 4.0
 
 
@@ -234,8 +240,9 @@
 
 
 def input_kernel(place, blocks, weight, mine, theirs, field):
-    filt = place[1]
-    for target, out in ((filt, mine), (filt ^ 2, theirs)):
+    core, filt = place[0], place[1]
+
+    def load(target):
         field[...] = jnp.zeros((256, 3 * lanes), f32)
         for j, other in enumerate(block_order):
             source = filt ^ other
@@ -247,30 +254,35 @@
                 inside = jnp.logical_and(row >= 0, row < rows)
                 piece = jnp.where(inside, blocks[j, :, pl.ds(at, lanes)] * scale, 0.0)
                 field[here, b * lanes : (b + 1) * lanes] = piece
-        total = jnp.zeros((3 * 128, 2 * lanes), f32)
+
+    def contract(planes_back):
+        total = jnp.zeros((len(planes_back) * 128, 2 * lanes), f32)
         for c in (-1, 0, 1):
             pair = split(shifted_columns(field[...], c))
             for b in (-1, 0, 1):
                 at = (1 - b) * lanes
                 window = jnp.concatenate([half[:, at : at + lanes] for half in pair], axis=1)
                 tap = 3 * (b + 1) + c + 1
-                taken = jnp.concatenate([weight[9 * a + tap] for a in range(3)], axis=0)
+                taken = jnp.concatenate([weight[9 * a + tap] for a in planes_back], axis=0)
                 total += jnp.dot(taken, window, preferred_element_type=f32)
-        total = (total[:, :lanes] + total[:, lanes:]).T
+        return (total[:, :lanes] + total[:, lanes:]).T
+
+    for target, out in ((filt, mine), (filt ^ 2, theirs)):
+        load(target)
+        total = contract((0, 1, 2))
         back, middle, ahead = total[:, :128], total[:, 128:256], total[:, 256:]
         out[0:cols] = middle[:cols] + back[cols:]
         out[cols:lanes] = middle[cols:] + ahead[:cols]
-        out[lanes : 3 * cols] = back[:cols]
-        out[3 * cols :] = ahead[cols:]
-
-
-def edge_kernel(place, mine, arrived, middle, keep, swap):
-    core = place[0]
+        out[lanes : 3 * cols] = jnp.where(core == 0, ahead[cols:], back[:cols])
+        load(target ^ 1)
+        rim = contract((jnp.where(core == 0, 2, 0),))
+        out[3 * cols :] = jnp.where(core == 0, rim[cols:], rim[:cols])
+
+
+def edge_kernel(mine, arrived, middle, rims):
     middle[...] = mine[0:lanes] + arrived[0:lanes]
-    low = mine[lanes : 3 * cols] + arrived[lanes : 3 * cols]
-    high = mine[3 * cols :] + arrived[3 * cols :]
-    keep[...] = jnp.where(core == 0, high, low)
-    swap[...] = jnp.where(core == 0, low, high)
+    rims[0] = mine[lanes : 3 * cols] + arrived[lanes : 3 * cols]
+    rims[1] = mine[3 * cols :] + arrived[3 * cols :]
 
 
 def rim_kernel(place, middle, here, there, out):
@@ -280,19 +292,29 @@
     out[cols:] = (middle[cols:] + high).astype(bf16)
 
 
-def gather_kernel(grad_scale, place, own, other, out):
+def turn_kernel(grad_scale, part, out):
+    power = [
+        jnp.broadcast_to(part[i, taps * block : taps * block + 1, 0:1], (block, 1)) for i in range(8)
+    ]
+    scale = jnp.exp2(jnp.concatenate(power, axis=0) - top) * grad_scale
+    for t in range(taps):
+        here = slice(t * block, (t + 1) * block)
+        out[t] = (part[:, here].reshape(128, 128) * scale).T
+
+
+def gather_kernel(grad_scale, place, own, part, out):
     core = place[0]
-    start = pl.program_id(0) * 9 * block
-    for part, side in ((own, core), (other, 1 - core)):
-        power = [
-            jnp.broadcast_to(part[i, taps * block : taps * block + 1, 0:1], (block, 1))
-            for i in range(8)
-        ]
-        scale = jnp.exp2(jnp.concatenate(power, axis=0) - top) * grad_scale
-        half = pl.ds(pl.multiple_of(side * 128, 128), 128)
-        for t in range(9):
-            here = pl.ds(pl.multiple_of(start + t * block, block), block)
-            out[t, :, half] = (part[:, here].reshape(128, 128) * scale).T
+    power = [
+        jnp.broadcast_to(part[i, taps * block : taps * block + 1, 0:1], (block, 1)) for i in range(8)
+    ]
+    scale = jnp.exp2(jnp.concatenate(power, axis=0) - top) * grad_scale
+    left = pl.ds(pl.multiple_of(core * 128, 128), 128)
+    right = pl.ds(pl.multiple_of((1 - core) * 128, 128), 128)
+    for t in range(9):
+        tap = pl.program_id(0) * 9 + t
+        here = pl.ds(pl.multiple_of(tap * block, block), block)
+        out[t, :, left] = own[tap]
+        out[t, :, right] = (part[:, here].reshape(128, 128) * scale).T
 
 
 def shards(cotangent, pre_act, layer_input, weight_one, weight_two):
@@ -365,8 +387,7 @@
         name="second",
     )(place, cot_cols, own_rows, other_rows)
     parts, _ = lax.optimization_barrier((parts, second))
-    rims = parts[:, :, voxels:]
-    other_rims = lax.ppermute(rims, "filt", core_swap).astype(f32)
+    other_rims = lax.ppermute(parts, "filt", core_swap)[:, :, voxels:].astype(f32)
     parts = parts.astype(f32)
     inputs = pl.pallas_call(
         inputs_kernel,
@@ -419,16 +440,15 @@
     near = jnp.broadcast_to(mine.astype(f16)[None], (16, share + 8, 128))
     near = lax.all_to_all(near, "slab", split_axis=0, concat_axis=0, tiled=True)
     near, arrived_x0 = lax.optimization_barrier((near, arrived_x0))
-    middle, keep, swap = pl.pallas_call(
+    middle, rims = pl.pallas_call(
         edge_kernel,
-        out_shape=[shape((lanes, 128), f32)] + [shape((cols, 128), f32)] * 2,
-        in_specs=[scalar_spec()] + whole(2),
-        out_specs=whole(3),
+        out_shape=[shape((lanes, 128), f32), shape((2, cols, 128), f32)],
+        in_specs=whole(2),
+        out_specs=whole(2),
         compiler_params=params(),
         name="edge",
-    )(place, mine_x0, arrived_x0)
-    swapped = lax.ppermute(swap, "filt", core_swap)
-    rims = lax.ppermute(jnp.stack([keep, swapped]), ("slab", "filt"), slab_step)
+    )(mine_x0, arrived_x0)
+    rims = lax.ppermute(rims, ("slab", "filt"), slab_step)
     other_rim = lax.ppermute(rims[1], "filt", core_swap)
     grad_x0 = pl.pallas_call(
         rim_kernel,
@@ -461,6 +481,15 @@
         power.astype(f32),
         own_wide,
     ).transpose(0, 2, 1)
+    turned = pl.pallas_call(
+        functools.partial(turn_kernel, grad_scale),
+        out_shape=shape((taps, 128, 128), f32),
+        in_specs=whole(1),
+        out_specs=whole(1)[0],
+        compiler_params=params(),
+        cost_estimate=cost(10**9, 1 << 20),
+        name="turn",
+    )(own_wide)
     grad_w1 = pl.pallas_call(
         functools.partial(gather_kernel, grad_scale),
         out_shape=shape((taps, 128, 256), f32),
@@ -469,7 +498,7 @@
         out_specs=pl.BlockSpec((9, 128, 256), lambda i: (i, 0, 0)),
         compiler_params=params(),
         name="gather",
-    )(place, own_wide, other_wide.astype(f32))
+    )(place, turned, other_wide.astype(f32))
     return (grad_w2, grad_w1, grad_x0)
 
 

time: 126 us -> 125 us (level)
  starting transfers between devices: 58 us -> 60.1 us
  waiting for transfers between devices: 37.2 us -> 35.4 us
    ppermute x1, starting transfers between devices: 0.01 us -> 6.28 us  [shards(): other_rim = lax.ppermute(rims[1], 'filt', core_swap)]
    ppermute x2 -> x1, starting transfers between devices: 7.57 us -> 3.31 us  [shards(): swapped = lax.ppermute(swap, 'filt', core_swap)]
  transfers between devices with their start and end apart: 20 -> 19, of which waited for: 13 -> 13; matrix products, arithmetic and copies ran while one was open for 3% -> 3% of each run, Pallas kernels for 9% -> 9%
where the time goes in v3:
time: 125 us; the launch traced here: 124 us
  starting transfers between devices  60.1 us (48%)
  waiting for transfers between devices  35.4 us (28%)
  Pallas kernels  17.3 us (14%)
  local copies, waits for them, and re-layouts  6.29 us (5%)
  other arithmetic  3.77 us (3%)
    all_to_all x1, starting transfers between devices, shards(): lax.all_to_all(merged, 'slab', split_axis=0, concat_axis=0, tiled=True)  12.9 us
    ppermute x1, waiting for transfers between devices, shards(): arrived_x0 = lax.ppermute(theirs_x0, 'filt', z_swap)  8.1 us
    all_to_all x1, waiting for transfers between devices, shards(): lax.all_to_all(merged, 'slab', split_axis=0, concat_axis=0, tiled=True)  6.9 us
    ppermute x1, starting transfers between devices, shards(): other_rim = lax.ppermute(rims[1], 'filt', core_swap)  6.28 us
    all_to_all x1, starting transfers between devices, shards(): lax.all_to_all(partial, 'filt', split_axis=0, concat_axis=0, tiled=True,...  5.34 us
    ppermute x3, waiting for transfers between devices, shards(): lax.ppermute(blocks, 'filt', [(i, i ^ swap) for i in range(16)])  4.96 us
    ppermute x1, waiting for transfers between devices, shards(): rims = lax.ppermute(rims, ('slab', 'filt'), slab_step)  4.71 us
    ppermute x1, starting transfers between devices, shards(): lax.ppermute(parts, 'filt', core_swap)[:, :, voxels:].astype(f32)  4.55 us
  transfers between devices with their start and end apart: 19, of which 13 were waited for; matrix products, arithmetic and copies ran while one was open for 3% of the time, Pallas kernels for 9%

profile of v3, /device:TPU:1, one launch (start us, length us, event | category | flops | bytes accessed | tf_op | source)
XLA Modules:
  0.0 123.8 jit_solution(11058336254448501736)
XLA Ops:
  3.1 3.3 %collective-permute-start.1 = (bf16[256,128]{1,0:T(8,128)(2,1)S(1)}, bf16[256,128]{1,0:T(8,128)(2,1)S(1)}, u32[]{:S(2)}, u32[]{:S(2)}) collective-permute-start(bf16[256,128]{1,0:T(8,128)(2,1)S(1)} %get-tuple-element.25.packed), channel_id=1, source_target_pairs={{0,1},{1,0},{2,3},{3,2},{4,5},{5,4},{6,7},{7,6},{8,9},{9,8},{10,11... | collective-permute-start | bytes 196616 | tf_op jit(solution)/shard_map/ppermute | solution.py:337
  7.3 1.3 %collective-permute-start.2 = (bf16[2,256,128]{2,1,0:T(8,128)(2,1)S(1)}, bf16[2,256,128]{2,1,0:T(8,128)(2,1)S(1)}, u32[]{:S(2)}, u32[]{:S(2)}) collective-permute-start(bf16[2,256,128]{2,1,0:T(8,128)(2,1)S(1)} %pad_maximum_fusion.2), channel_id=1, source_target_pairs={{0,16},{2,18},{4,20},{6,22},{8,24},{10,26},{12,28},{14,30},{16,32}... | collective-permute-start | bytes 393224 | tf_op jit(solution)/shard_map/ppermute | solution.py:338
  11.2 3.6 %all-to-all-start.1 = ((bf16[8,3,128,128]{3,2,1,0:T(8,128)(2,1)}), bf16[8,3,128,128]{3,2,1,0:T(8,128)(2,1)S(1)}, u32[]{:S(2)}, u32[]{:S(2)}) async-start(bf16[8,3,128,128]{3,2,1,0:T(8,128)(2,1)} %message.1), calls=%async_computation.1 | async-start | bytes 1572864 | tf_op jit(solution)/shard_map/all_to_all | solution.py:348
  15.3 4.1 %collective-permute-start.3 = (bf16[2,256,128]{2,1,0:T(8,128)(2,1)S(1)}, bf16[2,256,128]{2,1,0:T(8,128)(2,1)S(1)}, u32[]{:S(2)}, u32[]{:S(2)}) collective-permute-start(bf16[2,256,128]{2,1,0:T(8,128)(2,1)S(1)} %collective-permute-done.2.ready.here), channel_id=1, source_target_pairs={{0,1},{1,0},{2,3},{3,2},{4,5},{5,4},{6,7},{7,6},{8,9},{9,8},{10,11... | collective-permute-start | bytes 393224 | tf_op jit(solution)/shard_map/ppermute | solution.py:339
  21.7 2.2 %back.1 = (f32[8,16,3200]{2,1,0:T(8,128)S(1)}, bf16[432,2048]{1,0:T(8,128)(2,1)S(1)}) custom-call(s32[3]{0:T(128)S(1)} %pad_add_fusion.place, bf16[2,16,16,64]{3,2,1,0:T(8,128)(2,1)S(1)} %bitcast.25, bf16[2,16,16,64]{3,2,1,0:T(8,128)(2,1)S(1)} %collective-permute-done.other, bf16[2,256,128]{2,1,0:T(8,128)(2,1)S(1)} %collective-permute-done.2.ready.here, ...), custom_call_target="tpu_custom_call" | custom-call | flops 10000000000 | bytes 4194304 | tf_op jit(solution)/shard_map/back/pallas_call | solution.py:363
  24.9 5.3 %all-to-all-start = ((f16[8,16,3200]{2,1,0:T(8,128)(2,1)}), f16[8,16,3200]{2,1,0:T(8,128)(2,1)}, u32[]{:S(2)}, u32[]{:S(2)}) async-start(f16[8,16,3200]{2,1,0:T(8,128)(2,1)} %convert_element_type.38), calls=%async_computation | async-start | bytes 1638400 | tf_op jit(solution)/shard_map/all_to_all | solution.py:375
  30.3 3.5 %collective-permute-start.5 = (bf16[8,3,128,128]{3,2,1,0:T(8,128)(2,1)S(1)}, bf16[8,3,128,128]{3,2,1,0:T(8,128)(2,1)S(1)}, u32[]{:S(2)}, u32[]{:S(2)}) collective-permute-start(bf16[8,3,128,128]{3,2,1,0:T(8,128)(2,1)S(1)} %all-to-all-done.1.own), channel_id=1, source_target_pairs={{0,1},{1,0},{2,3},{3,2},{4,5},{5,4},{6,7},{7,6},{8,9},{9,8},{10,11... | collective-permute-start | bytes 2359304 | tf_op jit(solution)/shard_map/ppermute | solution.py:378
  33.8 1.9 %collective-permute-done.5.other = bf16[8,3,128,128]{3,2,1,0:T(8,128)(2,1)S(1)} collective-permute-done((bf16[8,3,128,128]{3,2,1,0:T(8,128)(2,1)S(1)}, bf16[8,3,128,128]{3,2,1,0:T(8,128)(2,1)S(1)}, u32[]{:S(2)}, u32[]{:S(2)}) %collective-permute-start.5) | collective-permute-done | bytes 786464 | tf_op jit(solution)/shard_map/ppermute | solution.py:378
  35.7 1.6 %second.1 = (f32[432,256]{1,0:T(8,128)S(1)}, f32[16,2048]{1,0:T(8,128)S(1)}) custom-call(s32[3]{0:T(128)S(1)} %pad_add_fusion.place, bf16[432,2048]{1,0:T(8,128)(2,1)S(1)} %get-tuple-element.29.cot_cols, bf16[8,3,128,128]{3,2,1,0:T(8,128)(2,1)S(1)} %all-to-all-done.1.own, bf16[8,3,128,128]{3,2,1,0:T(8,128)(2,1)S(1)} %collective-permute-done.5.other), custom_call_target="tpu_custom_call" | custom-call | flops 452984832 | bytes 6291456 | tf_op jit(solution)/shard_map/second/pallas_call | solution.py:379
  38.1 2.0 %all-to-all-done = f16[8,16,3200]{2,1,0:T(8,128)(2,1)} async-done(((f16[8,16,3200]{2,1,0:T(8,128)(2,1)}), f16[8,16,3200]{2,1,0:T(8,128)(2,1)}, u32[]{:S(2)}, u32[]{:S(2)}) %all-to-all-start) | async-done | bytes 819232 | tf_op jit(solution)/shard_map/all_to_all | solution.py:375
  40.1 4.5 %collective-permute-start.6 = (f16[8,16,3200]{2,1,0:T(8,128)(2,1)}, f16[8,16,3200]{2,1,0:T(8,128)(2,1)S(1)}, u32[]{:S(2)}, u32[]{:S(2)}) collective-permute-start(f16[8,16,3200]{2,1,0:T(8,128)(2,1)} %all-to-all-done), channel_id=1, source_target_pairs={{0,1},{1,0},{2,3},{3,2},{4,5},{5,4},{6,7},{7,6},{8,9},{9,8},{10,11... | collective-permute-start | bytes 2457608 | tf_op jit(solution)/shard_map/ppermute | solution.py:390
  50.1 12.9 %all-to-all-start.2 = ((f16[16,96,128]{2,1,0:T(8,128)(2,1)}), f16[16,96,128]{2,1,0:T(8,128)(2,1)S(1)}, u32[]{:S(2)}, u32[]{:S(2)}) async-start(f16[16,96,128]{2,1,0:T(8,128)(2,1)} %convert_element_type.41), calls=%async_computation.2 | async-start | bytes 786432 | tf_op jit(solution)/shard_map/all_to_all | solution.py:413
  64.0 5.0 %collective-permute-done.8 = f16[2,16,2176]{2,1,0:T(8,128)(2,1)S(1)} collective-permute-done((f16[2,16,2176]{2,1,0:T(8,128)(2,1)S(1)}, f16[2,16,2176]{2,1,0:T(8,128)(2,1)S(1)}, u32[]{:S(2)}, u32[]{:S(2)}) %collective-permute-start.8) | collective-permute-done | bytes 139296 | tf_op jit(solution)/shard_map/ppermute | solution.py:418
  69.0 1.6 %collective-permute-start.9 = (f16[4,16,2176]{2,1,0:T(8,128)(2,1)S(1)}, f16[4,16,2176]{2,1,0:T(8,128)(2,1)S(1)}, u32[]{:S(2)}, u32[]{:S(2)}) collective-permute-start(f16[4,16,2176]{2,1,0:T(8,128)(2,1)S(1)} %pad_maximum_fusion), channel_id=1, source_target_pairs={{0,1},{1,0},{2,3},{3,2},{4,5},{5,4},{6,7},{7,6},{8,9},{9,8},{10,11... | collective-permute-start | bytes 835592 | tf_op jit(solution)/shard_map/ppermute | solution.py:418
  70.6 6.9 %all-to-all-done.2 = f16[16,96,128]{2,1,0:T(8,128)(2,1)S(1)} async-done(((f16[16,96,128]{2,1,0:T(8,128)(2,1)}), f16[16,96,128]{2,1,0:T(8,128)(2,1)S(1)}, u32[]{:S(2)}, u32[]{:S(2)}) %all-to-all-start.2) | async-done | bytes 393248 | tf_op jit(solution)/shard_map/all_to_all | solution.py:413
  79.1 4.1 %all-to-all-start.3 = ((f16[16,96,128]{2,1,0:T(8,128)(2,1)}), f16[16,96,128]{2,1,0:T(8,128)(2,1)S(1)}, u32[]{:S(2)}, u32[]{:S(2)}) async-start(f16[16,96,128]{2,1,0:T(8,128)(2,1)} %broadcast_in_dim.6), calls=%async_computation.3 | async-start | bytes 786432 | tf_op jit(solution)/shard_map/all_to_all | solution.py:441
  83.4 2.4 %input.1 = (f32[256,128]{1,0:T(8,128)S(1)}, f32[256,128]{1,0:T(8,128)S(1)}) custom-call(s32[3]{0:T(128)S(1)} %pad_add_fusion.place, f32[8,16,2176]{2,1,0:T(8,128)S(1)} %maximum_convert_fusion.blocks, bf16[27,128,256]{2,1,0:T(8,128)(2,1)S(1)} %copy-done.7), custom_call_target="tpu_custom_call" | custom-call | flops 905969664 | bytes 4194304 | tf_op jit(solution)/shard_map/input/pallas_call | solution.py:421
  86.8 8.1 %collective-permute-done.10.arrived = f32[256,128]{1,0:T(8,128)S(1)} collective-permute-done((f32[256,128]{1,0:T(8,128)S(1)}, f32[256,128]{1,0:T(8,128)S(1)}, u32[]{:S(2)}, u32[]{:S(2)}) %collective-permute-start.10) | collective-permute-done | bytes 131104 | tf_op jit(solution)/shard_map/ppermute | solution.py:431
  94.9 2.2 %all-to-all-done.3 = f16[16,96,128]{2,1,0:T(8,128)(2,1)S(1)} async-done(((f16[16,96,128]{2,1,0:T(8,128)(2,1)}), f16[16,96,128]{2,1,0:T(8,128)(2,1)S(1)}, u32[]{:S(2)}, u32[]{:S(2)}) %all-to-all-start.3) | async-done | bytes 393248 | tf_op jit(solution)/shard_map/all_to_all | solution.py:441
  98.3 4.2 %all-to-all-start.4 = ((f16[8,440,128]{2,1,0:T(8,128)(2,1)}), f16[8,440,128]{2,1,0:T(8,128)(2,1)S(1)}, u32[]{:S(2)}, u32[]{:S(2)}) async-start(f16[8,440,128]{2,1,0:T(8,128)(2,1)} %broadcast_in_dim.8), calls=%async_computation.4 | async-start | bytes 1802240 | tf_op jit(solution)/shard_map/all_to_all | solution.py:465
  103.9 4.7 %collective-permute-done.11.here = f32[2,64,128]{2,1,0:T(8,128)S(1)} collective-permute-done((f32[2,64,128]{2,1,0:T(8,128)S(1)}, f32[2,64,128]{2,1,0:T(8,128)S(1)}, u32[]{:S(2)}, u32[]{:S(2)}) %collective-permute-start.11) | collective-permute-done | bytes 65568 | tf_op jit(solution)/shard_map/ppermute | solution.py:451
  108.6 6.3 %collective-permute-start.12 = (f32[64,128]{1,0:T(8,128)S(1)}, f32[64,128]{1,0:T(8,128)S(1)}, u32[]{:S(2)}, u32[]{:S(2)}) collective-permute-start(f32[64,128]{1,0:T(8,128)S(1)} %slice_bitcast_fusion), channel_id=1, source_target_pairs={{0,1},{1,0},{2,3},{3,2},{4,5},{5,4},{6,7},{7,6},{8,9},{9,8},{10,11... | collective-permute-start | bytes 98312 | tf_op jit(solution)/shard_map/ppermute | solution.py:452
  116.9 1.5 %collective-permute-start.13 = (f16[8,440,128]{2,1,0:T(8,128)(2,1)S(1)}, f16[8,440,128]{2,1,0:T(8,128)(2,1)S(1)}, u32[]{:S(2)}, u32[]{:S(2)}) collective-permute-start(f16[8,440,128]{2,1,0:T(8,128)(2,1)S(1)} %all-to-all-done.4), channel_id=1, source_target_pairs={{0,1},{1,0},{2,3},{3,2},{4,5},{5,4},{6,7},{7,6},{8,9},{9,8},{10,11... | collective-permute-start | bytes 2703368 | tf_op jit(solution)/shard_map/ppermute | solution.py:469
  120.6 3.3 %gather.1 = f32[27,128,256]{2,1,0:T(8,128)} custom-call(s32[3]{0:T(128)S(1)} %pad_add_fusion.place, f32[27,128,128]{2,1,0:T(8,128)S(1)} %turn.1.own, f32[8,440,128]{2,1,0:T(8,128)S(1)} %convert_element_type.50.part), custom_call_target="tpu_custom_call" | custom-call | tf_op jit(solution)/shard_map/gather/pallas_call | solution.py:493
  (69 shorter events, 26.2 us)
Async XLA Ops:
  0.7 0.9 copy-start.2
  2.4 17.1 %copy-start.8 = (bf16[27,256,16]{1,2,0:T(8,128)(2,1)S(1)}, bf16[27,256,16]{1,2,0:T(8,128)(2,1)}, u32[]{:S(2)}) copy-start(bf16[27,256,16]{1,2,0:T(8,128)(2,1)} %param.9) | copy-start | bytes 663556
  3.1 4.2 %collective-permute-start.1 = (bf16[256,128]{1,0:T(8,128)(2,1)S(1)}, bf16[256,128]{1,0:T(8,128)(2,1)S(1)}, u32[]{:S(2)}, u32[]{:S(2)}) collective-permute-start(bf16[256,128]{1,0:T(8,128)(2,1)S(1)} %get-tuple-element.25.packed), channel_id=1, source_target_pairs={{0,1},{1,0},{2,3},{3,2},{4,5},{5,4},{6,7},{7,6},{8,9},{9,8},{10,11... | collective-permute-start | bytes 196616 | tf_op jit(solution)/shard_map/ppermute | solution.py:337
  7.3 8.0 %collective-permute-start.2 = (bf16[2,256,128]{2,1,0:T(8,128)(2,1)S(1)}, bf16[2,256,128]{2,1,0:T(8,128)(2,1)S(1)}, u32[]{:S(2)}, u32[]{:S(2)}) collective-permute-start(bf16[2,256,128]{2,1,0:T(8,128)(2,1)S(1)} %pad_maximum_fusion.2), channel_id=1, source_target_pairs={{0,16},{2,18},{4,20},{6,22},{8,24},{10,26},{12,28},{14,30},{16,32}... | collective-permute-start | bytes 393224 | tf_op jit(solution)/shard_map/ppermute | solution.py:338
  11.2 13.8 %all-to-all-start.1 = ((bf16[8,3,128,128]{3,2,1,0:T(8,128)(2,1)}), bf16[8,3,128,128]{3,2,1,0:T(8,128)(2,1)S(1)}, u32[]{:S(2)}, u32[]{:S(2)}) async-start(bf16[8,3,128,128]{3,2,1,0:T(8,128)(2,1)} %message.1), calls=%async_computation.1 | async-start | bytes 1572864 | tf_op jit(solution)/shard_map/all_to_all | solution.py:348
  15.3 6.4 %collective-permute-start.3 = (bf16[2,256,128]{2,1,0:T(8,128)(2,1)S(1)}, bf16[2,256,128]{2,1,0:T(8,128)(2,1)S(1)}, u32[]{:S(2)}, u32[]{:S(2)}) collective-permute-start(bf16[2,256,128]{2,1,0:T(8,128)(2,1)S(1)} %collective-permute-done.2.ready.here), channel_id=1, source_target_pairs={{0,1},{1,0},{2,3},{3,2},{4,5},{5,4},{6,7},{7,6},{8,9},{9,8},{10,11... | collective-permute-start | bytes 393224 | tf_op jit(solution)/shard_map/ppermute | solution.py:339
  19.4 0.9 copy-start.3
  20.1 1.6 %collective-permute-start.4 = (bf16[128,432]{1,0:T(8,128)(2,1)S(1)}, bf16[128,432]{1,0:T(8,128)(2,1)S(1)}, u32[]{:S(2)}, u32[]{:S(2)}) collective-permute-start(bf16[128,432]{1,0:T(8,128)(2,1)S(1)} %get-tuple-element.27), channel_id=1, source_target_pairs={{0,1},{1,0},{2,3},{3,2},{4,5},{5,4},{6,7},{7,6},{8,9},{9,8},{10,11... | collective-permute-start | bytes 331784 | tf_op jit(solution)/shard_map/ppermute | solution.py:361
  20.3 1.4 %collective-permute-start = (bf16[2,16,16,64]{3,2,1,0:T(8,128)(2,1)S(1)}, bf16[2,16,16,64]{3,2,1,0:T(8,128)(2,1)S(1)}, u32[]{:S(2)}, u32[]{:S(2)}) collective-permute-start(bf16[2,16,16,64]{3,2,1,0:T(8,128)(2,1)S(1)} %bitcast.24), channel_id=1, source_target_pairs={{0,1},{1,0},{2,3},{3,2},{4,5},{5,4},{6,7},{7,6},{8,9},{9,8},{10,11... | collective-permute-start | bytes 196616 | tf_op jit(solution)/shard_map/ppermute | solution.py:351
  24.9 15.2 %all-to-all-start = ((f16[8,16,3200]{2,1,0:T(8,128)(2,1)}), f16[8,16,3200]{2,1,0:T(8,128)(2,1)}, u32[]{:S(2)}, u32[]{:S(2)}) async-start(f16[8,16,3200]{2,1,0:T(8,128)(2,1)} %convert_element_type.38), calls=%async_computation | async-start | bytes 1638400 | tf_op jit(solution)/shard_map/all_to_all | solution.py:375
  30.3 5.4 %collective-permute-start.5 = (bf16[8,3,128,128]{3,2,1,0:T(8,128)(2,1)S(1)}, bf16[8,3,128,128]{3,2,1,0:T(8,128)(2,1)S(1)}, u32[]{:S(2)}, u32[]{:S(2)}) collective-permute-start(bf16[8,3,128,128]{3,2,1,0:T(8,128)(2,1)S(1)} %all-to-all-done.1.own), channel_id=1, source_target_pairs={{0,1},{1,0},{2,3},{3,2},{4,5},{5,4},{6,7},{7,6},{8,9},{9,8},{10,11... | collective-permute-start | bytes 2359304 | tf_op jit(solution)/shard_map/ppermute | solution.py:378
  40.1 6.7 %collective-permute-start.6 = (f16[8,16,3200]{2,1,0:T(8,128)(2,1)}, f16[8,16,3200]{2,1,0:T(8,128)(2,1)S(1)}, u32[]{:S(2)}, u32[]{:S(2)}) collective-permute-start(f16[8,16,3200]{2,1,0:T(8,128)(2,1)} %all-to-all-done), channel_id=1, source_target_pairs={{0,1},{1,0},{2,3},{3,2},{4,5},{5,4},{6,7},{7,6},{8,9},{9,8},{10,11... | collective-permute-start | bytes 2457608 | tf_op jit(solution)/shard_map/ppermute | solution.py:390
  46.9 1.0 copy-start.1
  49.2 13.8 %collective-permute-start.7 = (f16[1,16,2176]{2,1,0:T(8,128)(2,1)S(1)}, f16[1,16,2176]{2,1,0:T(8,128)(2,1)S(1)}, u32[]{:S(2)}, u32[]{:S(2)}) collective-permute-start(f16[1,16,2176]{2,1,0:T(8,128)(2,1)S(1)} %convert_bitcast_fusion), channel_id=1, source_target_pairs={{0,4},{1,5},{2,6},{3,7},{4,0},{5,1},{6,2},{7,3},{8,12},{9,13},{10,... | collective-permute-start | bytes 208904 | tf_op jit(solution)/shard_map/ppermute | solution.py:418
  50.1 27.4 %all-to-all-start.2 = ((f16[16,96,128]{2,1,0:T(8,128)(2,1)}), f16[16,96,128]{2,1,0:T(8,128)(2,1)S(1)}, u32[]{:S(2)}, u32[]{:S(2)}) async-start(f16[16,96,128]{2,1,0:T(8,128)(2,1)} %convert_element_type.41), calls=%async_computation.2 | async-start | bytes 786432 | tf_op jit(solution)/shard_map/all_to_all | solution.py:413
  63.1 5.9 %collective-permute-start.8 = (f16[2,16,2176]{2,1,0:T(8,128)(2,1)S(1)}, f16[2,16,2176]{2,1,0:T(8,128)(2,1)S(1)}, u32[]{:S(2)}, u32[]{:S(2)}) collective-permute-start(f16[2,16,2176]{2,1,0:T(8,128)(2,1)S(1)} %pad_maximum_fusion.1), channel_id=1, source_target_pairs={{0,12},{1,13},{2,14},{3,15},{4,8},{5,9},{6,10},{7,11},{8,4},{9,5},... | collective-permute-start | bytes 417800 | tf_op jit(solution)/shard_map/ppermute | solution.py:418
  69.0 14.2 %collective-permute-start.9 = (f16[4,16,2176]{2,1,0:T(8,128)(2,1)S(1)}, f16[4,16,2176]{2,1,0:T(8,128)(2,1)S(1)}, u32[]{:S(2)}, u32[]{:S(2)}) collective-permute-start(f16[4,16,2176]{2,1,0:T(8,128)(2,1)S(1)} %pad_maximum_fusion), channel_id=1, source_target_pairs={{0,1},{1,0},{2,3},{3,2},{4,5},{5,4},{6,7},{7,6},{8,9},{9,8},{10,11... | collective-permute-start | bytes 835592 | tf_op jit(solution)/shard_map/ppermute | solution.py:418
  77.6 5.8 %copy-start.7 = (bf16[27,128,256]{2,1,0:T(8,128)(2,1)S(1)}, bf16[27,128,256]{2,1,0:T(8,128)(2,1)}, u32[]{:S(2)}) copy-start(bf16[27,128,256]{2,1,0:T(8,128)(2,1)} %weight.1) | copy-start | bytes 5308420
  79.1 18.0 %all-to-all-start.3 = ((f16[16,96,128]{2,1,0:T(8,128)(2,1)}), f16[16,96,128]{2,1,0:T(8,128)(2,1)S(1)}, u32[]{:S(2)}, u32[]{:S(2)}) async-start(f16[16,96,128]{2,1,0:T(8,128)(2,1)} %broadcast_in_dim.6), calls=%async_computation.3 | async-start | bytes 786432 | tf_op jit(solution)/shard_map/all_to_all | solution.py:441
  85.8 9.1 %collective-permute-start.10 = (f32[256,128]{1,0:T(8,128)S(1)}, f32[256,128]{1,0:T(8,128)S(1)}, u32[]{:S(2)}, u32[]{:S(2)}) collective-permute-start(f32[256,128]{1,0:T(8,128)S(1)} %get-tuple-element.37), channel_id=1, source_target_pairs={{0,2},{1,3},{2,0},{3,1},{4,6},{5,7},{6,4},{7,5},{8,10},{9,11},{10,... | collective-permute-start | bytes 393224 | tf_op jit(solution)/shard_map/ppermute | solution.py:431
  98.3 18.6 %all-to-all-start.4 = ((f16[8,440,128]{2,1,0:T(8,128)(2,1)}), f16[8,440,128]{2,1,0:T(8,128)(2,1)S(1)}, u32[]{:S(2)}, u32[]{:S(2)}) async-start(f16[8,440,128]{2,1,0:T(8,128)(2,1)} %broadcast_in_dim.8), calls=%async_computation.4 | async-start | bytes 1802240 | tf_op jit(solution)/shard_map/all_to_all | solution.py:465
  102.6 6.0 %collective-permute-start.11 = (f32[2,64,128]{2,1,0:T(8,128)S(1)}, f32[2,64,128]{2,1,0:T(8,128)S(1)}, u32[]{:S(2)}, u32[]{:S(2)}) collective-permute-start(f32[2,64,128]{2,1,0:T(8,128)S(1)} %get-tuple-element.42), channel_id=1, source_target_pairs={{0,16},{2,18},{4,20},{6,22},{8,24},{10,26},{12,28},{14,30},{16,32}... | collective-permute-start | bytes 196616 | tf_op jit(solution)/shard_map/ppermute | solution.py:451
  108.6 7.1 %collective-permute-start.12 = (f32[64,128]{1,0:T(8,128)S(1)}, f32[64,128]{1,0:T(8,128)S(1)}, u32[]{:S(2)}, u32[]{:S(2)}) collective-permute-start(f32[64,128]{1,0:T(8,128)S(1)} %slice_bitcast_fusion), channel_id=1, source_target_pairs={{0,1},{1,0},{2,3},{3,2},{4,5},{5,4},{6,7},{7,6},{8,9},{9,8},{10,11... | collective-permute-start | bytes 98312 | tf_op jit(solution)/shard_map/ppermute | solution.py:452
  116.9 3.6 %collective-permute-start.13 = (f16[8,440,128]{2,1,0:T(8,128)(2,1)S(1)}, f16[8,440,128]{2,1,0:T(8,128)(2,1)S(1)}, u32[]{:S(2)}, u32[]{:S(2)}) collective-permute-start(f16[8,440,128]{2,1,0:T(8,128)(2,1)S(1)} %all-to-all-done.4), channel_id=1, source_target_pairs={{0,1},{1,0},{2,3},{3,2},{4,5},{5,4},{6,7},{7,6},{8,9},{9,8},{10,11... | collective-permute-start | bytes 2703368 | tf_op jit(solution)/shard_map/ppermute | solution.py:469
  (4 other events, 3.1 us)

commit v4 on v3

--- a/solution.py
+++ b/solution.py
@@ -31,8 +31,8 @@
 slab_step += [((s + 1) * 16 + f, s * 16 + f) for s in range(15) for f in range(1, 16, 2)]
 
 
-def params():
-    return pltpu.CompilerParams(vmem_limit_bytes=48 * 1024 * 1024)
+def params(limit=48):
+    return pltpu.CompilerParams(vmem_limit_bytes=limit * 1024 * 1024)
 
 
 def cost(flops, moved):
@@ -74,7 +74,20 @@
         out[...] = jnp.concatenate([field, side], axis=1)
 
 
-def message_kernel(pre, x, packed, out):
+def stack_kernel(keep, swapped, ready, out):
+    out[0] = keep[...]
+    out[1] = swapped[...]
+
+
+def message_kernel(far_pre, far_x, packed, out, pre, x, sems):
+    copies = [
+        pltpu.make_async_copy(far_pre, pre, sems.at[0]),
+        pltpu.make_async_copy(far_x, x, sems.at[1]),
+    ]
+    for copy in copies:
+        copy.start()
+    for copy in copies:
+        copy.wait()
     value = pre[...].astype(f32).reshape(lanes, 256)
     active = jnp.where(value > 0, value, leak_slope * value).astype(bf16)
     own = x[...].reshape(lanes, 128)
@@ -335,16 +348,29 @@
         name="pack",
     )(place, cot, x)
     swapped = lax.ppermute(swap, "filt", core_swap)
-    here = lax.ppermute(jnp.stack([keep, swapped]), ("slab", "filt"), slab_step)
-    there = lax.ppermute(here, "filt", core_swap)
     message = pl.pallas_call(
         message_kernel,
         out_shape=shape((8, 3, 128, 128), bf16),
-        in_specs=[pl.BlockSpec()] * 2 + [pl.BlockSpec(memory_space=pl.ANY)],
-        out_specs=whole(1)[0],
-        compiler_params=params(),
+        in_specs=[pl.BlockSpec(memory_space=pl.ANY)] * 3,
+        out_specs=whole(1)[0],
+        scratch_shapes=[
+            pltpu.VMEM((planes, cols, 256), bf16),
+            pltpu.VMEM((planes, cols, 128), bf16),
+            pltpu.SemaphoreType.DMA((2,)),
+        ],
+        compiler_params=params(60),
         name="message",
     )(pre, x, swap)
+    both = pl.pallas_call(
+        stack_kernel,
+        out_shape=shape((2, 256, 128), bf16),
+        in_specs=whole(2) + [pl.BlockSpec(memory_space=pl.ANY)],
+        out_specs=whole(1)[0],
+        compiler_params=params(),
+        name="stack",
+    )(keep, swapped, message)
+    here = lax.ppermute(both, ("slab", "filt"), slab_step)
+    there = lax.ppermute(here, "filt", core_swap)
     own_rows = lax.all_to_all(
         message, "filt", split_axis=0, concat_axis=0, tiled=True, axis_index_groups=same_core
     )

time: 125 us -> 124 us (level)
  starting transfers between devices: 60.1 us -> 57.6 us
  waiting for transfers between devices: 35.4 us -> 36.8 us
    ppermute x1, waiting for transfers between devices: 0.5 us -> 3.11 us  [shards(): here = lax.ppermute(both, ('slab', 'filt'), slab_step)]
    ppermute x1, starting transfers between devices: 4.11 us -> 1.69 us  [shards(): there = lax.ppermute(here, 'filt', core_swap)]
  transfers between devices with their start and end apart: 19 -> 19, of which waited for: 13 -> 12; matrix products, arithmetic and copies ran while one was open for 3% -> 4% of each run, Pallas kernels for 9% -> 10%
where the time goes in v4:
time: 124 us; the launch traced here: 123 us
  starting transfers between devices  57.6 us (46%)
  waiting for transfers between devices  36.8 us (30%)
  Pallas kernels  18.4 us (15%)
  local copies, waits for them, and re-layouts  5.83 us (5%)
  other arithmetic  3.76 us (3%)
    all_to_all x1, starting transfers between devices, shards(): lax.all_to_all(merged, 'slab', split_axis=0, concat_axis=0, tiled=True)  12.8 us
    ppermute x1, waiting for transfers between devices, shards(): arrived_x0 = lax.ppermute(theirs_x0, 'filt', z_swap)  7.92 us
    all_to_all x1, waiting for transfers between devices, shards(): lax.all_to_all(merged, 'slab', split_axis=0, concat_axis=0, tiled=True)  6.9 us
    ppermute x1, starting transfers between devices, shards(): other_rim = lax.ppermute(rims[1], 'filt', core_swap)  6.27 us
    all_to_all x1, starting transfers between devices, shards(): lax.all_to_all(partial, 'filt', split_axis=0, concat_axis=0, tiled=True,...  5.33 us
    ppermute x3, waiting for transfers between devices, shards(): lax.ppermute(blocks, 'filt', [(i, i ^ swap) for i in range(16)])  4.96 us
    ppermute x1, waiting for transfers between devices, shards(): rims = lax.ppermute(rims, ('slab', 'filt'), slab_step)  4.71 us
    ppermute x1, starting transfers between devices, shards(): lax.ppermute(parts, 'filt', core_swap)[:, :, voxels:].astype(f32)  4.55 us
  transfers between devices with their start and end apart: 19, of which 12 were waited for; matrix products, arithmetic and copies ran while one was open for 4% of the time, Pallas kernels for 10%

profile of v4, /device:TPU:1, one launch (start us, length us, event | category | flops | bytes accessed | tf_op | source)
XLA Modules:
  0.0 123.4 jit_solution(1002631564454170262)
XLA Ops:
  3.1 3.3 %collective-permute-start.1 = (bf16[256,128]{1,0:T(8,128)(2,1)S(1)}, bf16[256,128]{1,0:T(8,128)(2,1)S(1)}, u32[]{:S(2)}, u32[]{:S(2)}) collective-permute-start(bf16[256,128]{1,0:T(8,128)(2,1)S(1)} %get-tuple-element.25.packed), channel_id=1, source_target_pairs={{0,1},{1,0},{2,3},{3,2},{4,5},{5,4},{6,7},{7,6},{8,9},{9,8},{10,11... | collective-permute-start | bytes 196616 | tf_op jit(solution)/shard_map/ppermute | solution.py:350
  6.4 1.9 %message.1.ready = bf16[8,3,128,128]{3,2,1,0:T(8,128)(2,1)} custom-call(bf16[2,64,256]{2,1,0:T(8,128)(2,1)} %bitcast.30, bf16[2,64,128]{2,1,0:T(8,128)(2,1)} %bitcast.24, bf16[256,128]{1,0:T(8,128)(2,1)} %copy-done.6), custom_call_target="tpu_custom_call" | custom-call | tf_op jit(solution)/shard_map/message/pallas_call | solution.py:351
  10.7 3.6 %all-to-all-start.1 = ((bf16[8,3,128,128]{3,2,1,0:T(8,128)(2,1)}), bf16[8,3,128,128]{3,2,1,0:T(8,128)(2,1)S(1)}, u32[]{:S(2)}, u32[]{:S(2)}) async-start(bf16[8,3,128,128]{3,2,1,0:T(8,128)(2,1)} %message.1.ready), calls=%async_computation.1 | async-start | bytes 1572864 | tf_op jit(solution)/shard_map/all_to_all | solution.py:374
  14.4 3.1 %collective-permute-done.2.ready.here = bf16[2,256,128]{2,1,0:T(8,128)(2,1)S(1)} collective-permute-done((bf16[2,256,128]{2,1,0:T(8,128)(2,1)S(1)}, bf16[2,256,128]{2,1,0:T(8,128)(2,1)S(1)}, u32[]{:S(2)}, u32[]{:S(2)}) %collective-permute-start.2) | collective-permute-done | bytes 131104 | tf_op jit(solution)/shard_map/ppermute | solution.py:372
  17.5 1.7 %collective-permute-start.3 = (bf16[2,256,128]{2,1,0:T(8,128)(2,1)S(1)}, bf16[2,256,128]{2,1,0:T(8,128)(2,1)S(1)}, u32[]{:S(2)}, u32[]{:S(2)}) collective-permute-start(bf16[2,256,128]{2,1,0:T(8,128)(2,1)S(1)} %collective-permute-done.2.ready.here), channel_id=1, source_target_pairs={{0,1},{1,0},{2,3},{3,2},{4,5},{5,4},{6,7},{7,6},{8,9},{9,8},{10,11... | collective-permute-start | bytes 393224 | tf_op jit(solution)/shard_map/ppermute | solution.py:373
  21.5 2.2 %back.1 = (f32[8,16,3200]{2,1,0:T(8,128)S(1)}, bf16[432,2048]{1,0:T(8,128)(2,1)S(1)}) custom-call(s32[3]{0:T(128)S(1)} %pad_add_fusion.place, bf16[2,16,16,64]{3,2,1,0:T(8,128)(2,1)S(1)} %bitcast.23, bf16[2,16,16,64]{3,2,1,0:T(8,128)(2,1)S(1)} %collective-permute-done.other, bf16[2,256,128]{2,1,0:T(8,128)(2,1)S(1)} %collective-permute-done.2.ready.here, ...), custom_call_target="tpu_custom_call" | custom-call | flops 10000000000 | bytes 4194304 | tf_op jit(solution)/shard_map/back/pallas_call | solution.py:389
  24.7 5.3 %all-to-all-start = ((f16[8,16,3200]{2,1,0:T(8,128)(2,1)}), f16[8,16,3200]{2,1,0:T(8,128)(2,1)}, u32[]{:S(2)}, u32[]{:S(2)}) async-start(f16[8,16,3200]{2,1,0:T(8,128)(2,1)} %convert_element_type.38), calls=%async_computation | async-start | bytes 1638400 | tf_op jit(solution)/shard_map/all_to_all | solution.py:401
  30.0 3.5 %collective-permute-start.5 = (bf16[8,3,128,128]{3,2,1,0:T(8,128)(2,1)S(1)}, bf16[8,3,128,128]{3,2,1,0:T(8,128)(2,1)S(1)}, u32[]{:S(2)}, u32[]{:S(2)}) collective-permute-start(bf16[8,3,128,128]{3,2,1,0:T(8,128)(2,1)S(1)} %all-to-all-done.1.own), channel_id=1, source_target_pairs={{0,1},{1,0},{2,3},{3,2},{4,5},{5,4},{6,7},{7,6},{8,9},{9,8},{10,11... | collective-permute-start | bytes 2359304 | tf_op jit(solution)/shard_map/ppermute | solution.py:404
  33.5 1.9 %collective-permute-done.5.other = bf16[8,3,128,128]{3,2,1,0:T(8,128)(2,1)S(1)} collective-permute-done((bf16[8,3,128,128]{3,2,1,0:T(8,128)(2,1)S(1)}, bf16[8,3,128,128]{3,2,1,0:T(8,128)(2,1)S(1)}, u32[]{:S(2)}, u32[]{:S(2)}) %collective-permute-start.5) | collective-permute-done | bytes 786464 | tf_op jit(solution)/shard_map/ppermute | solution.py:404
  35.5 1.6 %second.1 = (f32[432,256]{1,0:T(8,128)S(1)}, f32[16,2048]{1,0:T(8,128)S(1)}) custom-call(s32[3]{0:T(128)S(1)} %pad_add_fusion.place, bf16[432,2048]{1,0:T(8,128)(2,1)S(1)} %get-tuple-element.29.cot_cols, bf16[8,3,128,128]{3,2,1,0:T(8,128)(2,1)S(1)} %all-to-all-done.1.own, bf16[8,3,128,128]{3,2,1,0:T(8,128)(2,1)S(1)} %collective-permute-done.5.other), custom_call_target="tpu_custom_call" | custom-call | flops 452984832 | bytes 6291456 | tf_op jit(solution)/shard_map/second/pallas_call | solution.py:405
  37.8 2.0 %all-to-all-done = f16[8,16,3200]{2,1,0:T(8,128)(2,1)} async-done(((f16[8,16,3200]{2,1,0:T(8,128)(2,1)}), f16[8,16,3200]{2,1,0:T(8,128)(2,1)}, u32[]{:S(2)}, u32[]{:S(2)}) %all-to-all-start) | async-done | bytes 819232 | tf_op jit(solution)/shard_map/all_to_all | solution.py:401
  39.9 4.6 %collective-permute-start.6 = (f16[8,16,3200]{2,1,0:T(8,128)(2,1)}, f16[8,16,3200]{2,1,0:T(8,128)(2,1)S(1)}, u32[]{:S(2)}, u32[]{:S(2)}) collective-permute-start(f16[8,16,3200]{2,1,0:T(8,128)(2,1)} %all-to-all-done), channel_id=1, source_target_pairs={{0,1},{1,0},{2,3},{3,2},{4,5},{5,4},{6,7},{7,6},{8,9},{9,8},{10,11... | collective-permute-start | bytes 2457608 | tf_op jit(solution)/shard_map/ppermute | solution.py:416
  49.8 12.8 %all-to-all-start.2 = ((f16[16,96,128]{2,1,0:T(8,128)(2,1)}), f16[16,96,128]{2,1,0:T(8,128)(2,1)S(1)}, u32[]{:S(2)}, u32[]{:S(2)}) async-start(f16[16,96,128]{2,1,0:T(8,128)(2,1)} %convert_element_type.41), calls=%async_computation.2 | async-start | bytes 786432 | tf_op jit(solution)/shard_map/all_to_all | solution.py:439
  63.6 5.0 %collective-permute-done.8 = f16[2,16,2176]{2,1,0:T(8,128)(2,1)S(1)} collective-permute-done((f16[2,16,2176]{2,1,0:T(8,128)(2,1)S(1)}, f16[2,16,2176]{2,1,0:T(8,128)(2,1)S(1)}, u32[]{:S(2)}, u32[]{:S(2)}) %collective-permute-start.8) | collective-permute-done | bytes 139296 | tf_op jit(solution)/shard_map/ppermute | solution.py:444
  68.6 1.6 %collective-permute-start.9 = (f16[4,16,2176]{2,1,0:T(8,128)(2,1)S(1)}, f16[4,16,2176]{2,1,0:T(8,128)(2,1)S(1)}, u32[]{:S(2)}, u32[]{:S(2)}) collective-permute-start(f16[4,16,2176]{2,1,0:T(8,128)(2,1)S(1)} %pad_maximum_fusion), channel_id=1, source_target_pairs={{0,1},{1,0},{2,3},{3,2},{4,5},{5,4},{6,7},{7,6},{8,9},{9,8},{10,11... | collective-permute-start | bytes 835592 | tf_op jit(solution)/shard_map/ppermute | solution.py:444
  70.2 6.9 %all-to-all-done.2 = f16[16,96,128]{2,1,0:T(8,128)(2,1)S(1)} async-done(((f16[16,96,128]{2,1,0:T(8,128)(2,1)}), f16[16,96,128]{2,1,0:T(8,128)(2,1)S(1)}, u32[]{:S(2)}, u32[]{:S(2)}) %all-to-all-start.2) | async-done | bytes 393248 | tf_op jit(solution)/shard_map/all_to_all | solution.py:439
  78.7 4.1 %all-to-all-start.3 = ((f16[16,96,128]{2,1,0:T(8,128)(2,1)}), f16[16,96,128]{2,1,0:T(8,128)(2,1)S(1)}, u32[]{:S(2)}, u32[]{:S(2)}) async-start(f16[16,96,128]{2,1,0:T(8,128)(2,1)} %broadcast_in_dim.6), calls=%async_computation.3 | async-start | bytes 786432 | tf_op jit(solution)/shard_map/all_to_all | solution.py:467
  83.0 2.6 %input.1 = (f32[256,128]{1,0:T(8,128)S(1)}, f32[256,128]{1,0:T(8,128)S(1)}) custom-call(s32[3]{0:T(128)S(1)} %pad_add_fusion.place, f32[8,16,2176]{2,1,0:T(8,128)S(1)} %maximum_convert_fusion.blocks, bf16[27,128,256]{2,1,0:T(8,128)(2,1)S(1)} %copy-done.7), custom_call_target="tpu_custom_call" | custom-call | flops 905969664 | bytes 4194304 | tf_op jit(solution)/shard_map/input/pallas_call | solution.py:447
  86.6 7.9 %collective-permute-done.10.arrived = f32[256,128]{1,0:T(8,128)S(1)} collective-permute-done((f32[256,128]{1,0:T(8,128)S(1)}, f32[256,128]{1,0:T(8,128)S(1)}, u32[]{:S(2)}, u32[]{:S(2)}) %collective-permute-start.10) | collective-permute-done | bytes 131104 | tf_op jit(solution)/shard_map/ppermute | solution.py:457
  94.5 2.2 %all-to-all-done.3 = f16[16,96,128]{2,1,0:T(8,128)(2,1)S(1)} async-done(((f16[16,96,128]{2,1,0:T(8,128)(2,1)}), f16[16,96,128]{2,1,0:T(8,128)(2,1)S(1)}, u32[]{:S(2)}, u32[]{:S(2)}) %all-to-all-start.3) | async-done | bytes 393248 | tf_op jit(solution)/shard_map/all_to_all | solution.py:467
  97.9 4.3 %all-to-all-start.4 = ((f16[8,440,128]{2,1,0:T(8,128)(2,1)}), f16[8,440,128]{2,1,0:T(8,128)(2,1)S(1)}, u32[]{:S(2)}, u32[]{:S(2)}) async-start(f16[8,440,128]{2,1,0:T(8,128)(2,1)} %broadcast_in_dim.8), calls=%async_computation.4 | async-start | bytes 1802240 | tf_op jit(solution)/shard_map/all_to_all | solution.py:491
  103.5 4.7 %collective-permute-done.11.here = f32[2,64,128]{2,1,0:T(8,128)S(1)} collective-permute-done((f32[2,64,128]{2,1,0:T(8,128)S(1)}, f32[2,64,128]{2,1,0:T(8,128)S(1)}, u32[]{:S(2)}, u32[]{:S(2)}) %collective-permute-start.11) | collective-permute-done | bytes 65568 | tf_op jit(solution)/shard_map/ppermute | solution.py:477
  108.2 6.3 %collective-permute-start.12 = (f32[64,128]{1,0:T(8,128)S(1)}, f32[64,128]{1,0:T(8,128)S(1)}, u32[]{:S(2)}, u32[]{:S(2)}) collective-permute-start(f32[64,128]{1,0:T(8,128)S(1)} %slice_bitcast_fusion), channel_id=1, source_target_pairs={{0,1},{1,0},{2,3},{3,2},{4,5},{5,4},{6,7},{7,6},{8,9},{9,8},{10,11... | collective-permute-start | bytes 98312 | tf_op jit(solution)/shard_map/ppermute | solution.py:478
  120.2 3.3 %gather.1 = f32[27,128,256]{2,1,0:T(8,128)} custom-call(s32[3]{0:T(128)S(1)} %pad_add_fusion.place, f32[27,128,128]{2,1,0:T(8,128)S(1)} %turn.1.own, f32[8,440,128]{2,1,0:T(8,128)S(1)} %convert_element_type.50.part), custom_call_target="tpu_custom_call" | custom-call | tf_op jit(solution)/shard_map/gather/pallas_call | solution.py:519
  (69 shorter events, 26.2 us)
Async XLA Ops:
  3.1 3.3 %copy-start.6 = (bf16[256,128]{1,0:T(8,128)(2,1)}, bf16[256,128]{1,0:T(8,128)(2,1)S(1)}, u32[]{:S(2)}) copy-start(bf16[256,128]{1,0:T(8,128)(2,1)S(1)} %get-tuple-element.25.packed) | copy-start | bytes 196612
  3.1 5.2 %collective-permute-start.1 = (bf16[256,128]{1,0:T(8,128)(2,1)S(1)}, bf16[256,128]{1,0:T(8,128)(2,1)S(1)}, u32[]{:S(2)}, u32[]{:S(2)}) collective-permute-start(bf16[256,128]{1,0:T(8,128)(2,1)S(1)} %get-tuple-element.25.packed), channel_id=1, source_target_pairs={{0,1},{1,0},{2,3},{3,2},{4,5},{5,4},{6,7},{7,6},{8,9},{9,8},{10,11... | collective-permute-start | bytes 196616 | tf_op jit(solution)/shard_map/ppermute | solution.py:350
  6.4 12.8 %copy-start.8 = (bf16[27,256,16]{1,2,0:T(8,128)(2,1)S(1)}, bf16[27,256,16]{1,2,0:T(8,128)(2,1)}, u32[]{:S(2)}) copy-start(bf16[27,256,16]{1,2,0:T(8,128)(2,1)} %param.9) | copy-start | bytes 663556
  8.3 1.1 copy-start
  9.4 8.1 %collective-permute-start.2 = (bf16[2,256,128]{2,1,0:T(8,128)(2,1)S(1)}, bf16[2,256,128]{2,1,0:T(8,128)(2,1)S(1)}, u32[]{:S(2)}, u32[]{:S(2)}) collective-permute-start(bf16[2,256,128]{2,1,0:T(8,128)(2,1)S(1)} %stack.17), channel_id=1, source_target_pairs={{0,16},{2,18},{4,20},{6,22},{8,24},{10,26},{12,28},{14,30},{16,32}... | collective-permute-start | bytes 393224 | tf_op jit(solution)/shard_map/ppermute | solution.py:372
  10.7 14.0 %all-to-all-start.1 = ((bf16[8,3,128,128]{3,2,1,0:T(8,128)(2,1)}), bf16[8,3,128,128]{3,2,1,0:T(8,128)(2,1)S(1)}, u32[]{:S(2)}, u32[]{:S(2)}) async-start(bf16[8,3,128,128]{3,2,1,0:T(8,128)(2,1)} %message.1.ready), calls=%async_computation.1 | async-start | bytes 1572864 | tf_op jit(solution)/shard_map/all_to_all | solution.py:374
  17.5 4.0 %collective-permute-start.3 = (bf16[2,256,128]{2,1,0:T(8,128)(2,1)S(1)}, bf16[2,256,128]{2,1,0:T(8,128)(2,1)S(1)}, u32[]{:S(2)}, u32[]{:S(2)}) collective-permute-start(bf16[2,256,128]{2,1,0:T(8,128)(2,1)S(1)} %collective-permute-done.2.ready.here), channel_id=1, source_target_pairs={{0,1},{1,0},{2,3},{3,2},{4,5},{5,4},{6,7},{7,6},{8,9},{9,8},{10,11... | collective-permute-start | bytes 393224 | tf_op jit(solution)/shard_map/ppermute | solution.py:373
  19.9 1.6 %collective-permute-start.4 = (bf16[128,432]{1,0:T(8,128)(2,1)S(1)}, bf16[128,432]{1,0:T(8,128)(2,1)S(1)}, u32[]{:S(2)}, u32[]{:S(2)}) collective-permute-start(bf16[128,432]{1,0:T(8,128)(2,1)S(1)} %get-tuple-element.27), channel_id=1, source_target_pairs={{0,1},{1,0},{2,3},{3,2},{4,5},{5,4},{6,7},{7,6},{8,9},{9,8},{10,11... | collective-permute-start | bytes 331784 | tf_op jit(solution)/shard_map/ppermute | solution.py:387
  20.1 1.4 %collective-permute-start = (bf16[2,16,16,64]{3,2,1,0:T(8,128)(2,1)S(1)}, bf16[2,16,16,64]{3,2,1,0:T(8,128)(2,1)S(1)}, u32[]{:S(2)}, u32[]{:S(2)}) collective-permute-start(bf16[2,16,16,64]{3,2,1,0:T(8,128)(2,1)S(1)} %bitcast.22), channel_id=1, source_target_pairs={{0,1},{1,0},{2,3},{3,2},{4,5},{5,4},{6,7},{7,6},{8,9},{9,8},{10,11... | collective-permute-start | bytes 196616 | tf_op jit(solution)/shard_map/ppermute | solution.py:377
  24.7 15.2 %all-to-all-start = ((f16[8,16,3200]{2,1,0:T(8,128)(2,1)}), f16[8,16,3200]{2,1,0:T(8,128)(2,1)}, u32[]{:S(2)}, u32[]{:S(2)}) async-start(f16[8,16,3200]{2,1,0:T(8,128)(2,1)} %convert_element_type.38), calls=%async_computation | async-start | bytes 1638400 | tf_op jit(solution)/shard_map/all_to_all | solution.py:401
  30.0 5.4 %collective-permute-start.5 = (bf16[8,3,128,128]{3,2,1,0:T(8,128)(2,1)S(1)}, bf16[8,3,128,128]{3,2,1,0:T(8,128)(2,1)S(1)}, u32[]{:S(2)}, u32[]{:S(2)}) collective-permute-start(bf16[8,3,128,128]{3,2,1,0:T(8,128)(2,1)S(1)} %all-to-all-done.1.own), channel_id=1, source_target_pairs={{0,1},{1,0},{2,3},{3,2},{4,5},{5,4},{6,7},{7,6},{8,9},{9,8},{10,11... | collective-permute-start | bytes 2359304 | tf_op jit(solution)/shard_map/ppermute | solution.py:404
  39.9 6.7 %collective-permute-start.6 = (f16[8,16,3200]{2,1,0:T(8,128)(2,1)}, f16[8,16,3200]{2,1,0:T(8,128)(2,1)S(1)}, u32[]{:S(2)}, u32[]{:S(2)}) collective-permute-start(f16[8,16,3200]{2,1,0:T(8,128)(2,1)} %all-to-all-done), channel_id=1, source_target_pairs={{0,1},{1,0},{2,3},{3,2},{4,5},{5,4},{6,7},{7,6},{8,9},{9,8},{10,11... | collective-permute-start | bytes 2457608 | tf_op jit(solution)/shard_map/ppermute | solution.py:416
  46.6 1.0 copy-start.2
  48.9 13.7 %collective-permute-start.7 = (f16[1,16,2176]{2,1,0:T(8,128)(2,1)S(1)}, f16[1,16,2176]{2,1,0:T(8,128)(2,1)S(1)}, u32[]{:S(2)}, u32[]{:S(2)}) collective-permute-start(f16[1,16,2176]{2,1,0:T(8,128)(2,1)S(1)} %convert_bitcast_fusion), channel_id=1, source_target_pairs={{0,4},{1,5},{2,6},{3,7},{4,0},{5,1},{6,2},{7,3},{8,12},{9,13},{10,... | collective-permute-start | bytes 208904 | tf_op jit(solution)/shard_map/ppermute | solution.py:444
  49.8 27.3 %all-to-all-start.2 = ((f16[16,96,128]{2,1,0:T(8,128)(2,1)}), f16[16,96,128]{2,1,0:T(8,128)(2,1)S(1)}, u32[]{:S(2)}, u32[]{:S(2)}) async-start(f16[16,96,128]{2,1,0:T(8,128)(2,1)} %convert_element_type.41), calls=%async_computation.2 | async-start | bytes 786432 | tf_op jit(solution)/shard_map/all_to_all | solution.py:439
  62.7 5.9 %collective-permute-start.8 = (f16[2,16,2176]{2,1,0:T(8,128)(2,1)S(1)}, f16[2,16,2176]{2,1,0:T(8,128)(2,1)S(1)}, u32[]{:S(2)}, u32[]{:S(2)}) collective-permute-start(f16[2,16,2176]{2,1,0:T(8,128)(2,1)S(1)} %pad_maximum_fusion.1), channel_id=1, source_target_pairs={{0,12},{1,13},{2,14},{3,15},{4,8},{5,9},{6,10},{7,11},{8,4},{9,5},... | collective-permute-start | bytes 417800 | tf_op jit(solution)/shard_map/ppermute | solution.py:444
  68.6 14.3 %collective-permute-start.9 = (f16[4,16,2176]{2,1,0:T(8,128)(2,1)S(1)}, f16[4,16,2176]{2,1,0:T(8,128)(2,1)S(1)}, u32[]{:S(2)}, u32[]{:S(2)}) collective-permute-start(f16[4,16,2176]{2,1,0:T(8,128)(2,1)S(1)} %pad_maximum_fusion), channel_id=1, source_target_pairs={{0,1},{1,0},{2,3},{3,2},{4,5},{5,4},{6,7},{7,6},{8,9},{9,8},{10,11... | collective-permute-start | bytes 835592 | tf_op jit(solution)/shard_map/ppermute | solution.py:444
  77.2 5.8 %copy-start.7 = (bf16[27,128,256]{2,1,0:T(8,128)(2,1)S(1)}, bf16[27,128,256]{2,1,0:T(8,128)(2,1)}, u32[]{:S(2)}) copy-start(bf16[27,128,256]{2,1,0:T(8,128)(2,1)} %weight.1) | copy-start | bytes 5308420
  78.7 17.9 %all-to-all-start.3 = ((f16[16,96,128]{2,1,0:T(8,128)(2,1)}), f16[16,96,128]{2,1,0:T(8,128)(2,1)S(1)}, u32[]{:S(2)}, u32[]{:S(2)}) async-start(f16[16,96,128]{2,1,0:T(8,128)(2,1)} %broadcast_in_dim.6), calls=%async_computation.3 | async-start | bytes 786432 | tf_op jit(solution)/shard_map/all_to_all | solution.py:467
  85.6 8.9 %collective-permute-start.10 = (f32[256,128]{1,0:T(8,128)S(1)}, f32[256,128]{1,0:T(8,128)S(1)}, u32[]{:S(2)}, u32[]{:S(2)}) collective-permute-start(f32[256,128]{1,0:T(8,128)S(1)} %get-tuple-element.37), channel_id=1, source_target_pairs={{0,2},{1,3},{2,0},{3,1},{4,6},{5,7},{6,4},{7,5},{8,10},{9,11},{10,... | collective-permute-start | bytes 393224 | tf_op jit(solution)/shard_map/ppermute | solution.py:457
  97.9 18.6 %all-to-all-start.4 = ((f16[8,440,128]{2,1,0:T(8,128)(2,1)}), f16[8,440,128]{2,1,0:T(8,128)(2,1)S(1)}, u32[]{:S(2)}, u32[]{:S(2)}) async-start(f16[8,440,128]{2,1,0:T(8,128)(2,1)} %broadcast_in_dim.8), calls=%async_computation.4 | async-start | bytes 1802240 | tf_op jit(solution)/shard_map/all_to_all | solution.py:491
  102.2 6.0 %collective-permute-start.11 = (f32[2,64,128]{2,1,0:T(8,128)S(1)}, f32[2,64,128]{2,1,0:T(8,128)S(1)}, u32[]{:S(2)}, u32[]{:S(2)}) collective-permute-start(f32[2,64,128]{2,1,0:T(8,128)S(1)} %get-tuple-element.42), channel_id=1, source_target_pairs={{0,16},{2,18},{4,20},{6,22},{8,24},{10,26},{12,28},{14,30},{16,32}... | collective-permute-start | bytes 196616 | tf_op jit(solution)/shard_map/ppermute | solution.py:477
  108.2 7.1 %collective-permute-start.12 = (f32[64,128]{1,0:T(8,128)S(1)}, f32[64,128]{1,0:T(8,128)S(1)}, u32[]{:S(2)}, u32[]{:S(2)}) collective-permute-start(f32[64,128]{1,0:T(8,128)S(1)} %slice_bitcast_fusion), channel_id=1, source_target_pairs={{0,1},{1,0},{2,3},{3,2},{4,5},{5,4},{6,7},{7,6},{8,9},{9,8},{10,11... | collective-permute-start | bytes 98312 | tf_op jit(solution)/shard_map/ppermute | solution.py:478
  116.5 3.6 %collective-permute-start.13 = (f16[8,440,128]{2,1,0:T(8,128)(2,1)S(1)}, f16[8,440,128]{2,1,0:T(8,128)(2,1)S(1)}, u32[]{:S(2)}, u32[]{:S(2)}) collective-permute-start(f16[8,440,128]{2,1,0:T(8,128)(2,1)S(1)} %all-to-all-done.4), channel_id=1, source_target_pairs={{0,1},{1,0},{2,3},{3,2},{4,5},{5,4},{6,7},{7,6},{8,9},{9,8},{10,11... | collective-permute-start | bytes 2703368 | tf_op jit(solution)/shard_map/ppermute | solution.py:495
  (4 other events, 3.3 us)
